TPU v7x, 32 devices: a whole 2x2x4 slice. The times are simulated.
32 devices in a mesh: seq: 8 (over z, y), expert: 4 (over x, core).
Axes of the slice: x: 2, y: 2, z: 4, core: 2. Of those that a mesh axis runs over, the one named last changes fastest.
Arguments:
- residual: bfloat16 [4096, 2304], P(('seq', 'expert')), may hold values from -6 to 6
- query_rows: bfloat16 [4096, 4096], P('seq', 'expert'), may hold values from -6 to 6
- key_rows: bfloat16 [4096, 4096], P('seq', 'expert'), may hold values from -6 to 6
- value_rows: bfloat16 [4096, 4096], P('seq', 'expert'), may hold values from -6 to 6
- log_decay: float32 [4096, 4096], P('seq', 'expert'), may hold values from -0.7 to 0
- write_rate: float32 [4096, 32], P('seq', 'expert'), may hold values from 0 to 1
- output_weight: bfloat16 [4096, 2304], P('expert'), may hold values from -0.09375 to 0.09375
- routes: int32 [4096, 8], P(('seq', 'expert')), may hold values from 0 to 31, all different within a row; in each aligned block of 128 rows (0 to 127, 128 to 255, ...) at most 64 rows name the same one
- route_gates: float32 [4096, 8], P(('seq', 'expert')), may hold values from 0.1 to 0.6
- expert_up: bfloat16 [32, 2304, 1024], P(('seq', 'expert')), may hold values from -0.125 to 0.125
- expert_down: bfloat16 [32, 512, 2304], P(('seq', 'expert')), may hold values from -0.25 to 0.25
Outputs:
- layer_out: bfloat16 [4096, 2304], P(('seq', 'expert'))
Inputs may be any that keep to these rules, and one draw needn't show every extreme that they name: `routes`: each row names 8 different experts. In each aligned block of 128 rows no expert is named by more than 64 rows, and in some block one expert is named by exactly 64.
All inputs are finite; a program needn't handle non-finite values.
Results may differ from a plain program's by a relative error of at most 0.007.
Values may be sent and summed in bfloat16 or wider, within the bound.
A program may use at most 128 MiB of HBM per device.

v0:
```python
import jax
import jax.numpy as jnp
from jax import lax
from jax.sharding import PartitionSpec as P

BLOCK = 64


precise = lax.Precision.HIGHEST


def unit_rows(block):
    return block * lax.rsqrt(jnp.sum(block * block, axis=-1, keepdims=True) + 1e-06)


def head_blocks(array, heads):
    tokens = array.shape[0]
    width = array.shape[1] // heads
    shaped = array.reshape(tokens // BLOCK, BLOCK, heads, width)
    return jnp.transpose(shaped, (2, 0, 1, 3))


def block_terms(query_rows, key_rows, value_rows, log_decay, write_rate):
    heads = write_rate.shape[1]
    queries = unit_rows(head_blocks(query_rows.astype(jnp.float32), heads))
    keyed = unit_rows(head_blocks(key_rows.astype(jnp.float32), heads))
    values = head_blocks(value_rows.astype(jnp.float32), heads)
    rates = head_blocks(write_rate, heads)[..., 0]
    summed = jnp.cumsum(head_blocks(log_decay, heads), axis=2)
    middle = summed[:, :, BLOCK // 2 - 1 : BLOCK // 2, :]
    rising = jnp.exp(summed - middle)
    falling = jnp.exp(middle - summed)
    total_decay = summed[:, :, BLOCK - 1 :, :]
    key_down = keyed * falling
    scores = jnp.einsum("hnsd,hntd->hnst", keyed * rising, key_down, precision=precise)
    positions = jnp.arange(BLOCK)
    strict = positions[:, None] > positions[None, :]
    causal = positions[:, None] >= positions[None, :]
    lower_part = jnp.where(strict, scores * rates[..., None], 0.0)
    system = lower_part + jnp.eye(BLOCK, dtype=jnp.float32)
    from_start = keyed * jnp.exp(summed)
    right_side = jnp.concatenate(
        [values * rates[..., None], from_start * rates[..., None]], axis=-1
    )
    solved = lax.linalg.triangular_solve(
        system, right_side, left_side=True, lower=True, unit_diagonal=True
    )
    value_width = values.shape[-1]
    fresh = solved[..., :value_width]
    carried = solved[..., value_width:]
    reach = jnp.where(
        causal, jnp.einsum("hnsd,hntd->hnst", queries * rising, key_down, precision=precise), 0.0
    )
    to_end = keyed * jnp.exp(total_decay - summed)
    key_width = keyed.shape[-1]
    transit = jnp.eye(key_width, dtype=jnp.float32) * jnp.exp(total_decay)[:, :, 0, :, None]
    transit = transit - jnp.einsum("hncd,hnce->hnde", to_end, carried, precision=precise)
    offset = jnp.einsum("hncd,hnce->hnde", to_end, fresh, precision=precise)
    exposure = queries * jnp.exp(summed) - jnp.einsum(
        "hnst,hntd->hnsd", reach, carried, precision=precise
    )
    direct = jnp.einsum("hnst,hnte->hnse", reach, fresh, precision=precise)
    return (transit, offset, exposure, direct)


def shard_chain(transit, offset, exposure, direct):
    heads = transit.shape[0]
    key_width = transit.shape[2]
    value_width = offset.shape[-1]
    identity_map = jnp.broadcast_to(
        jnp.eye(key_width, dtype=jnp.float32), (heads, key_width, key_width)
    )
    start = (identity_map, jnp.zeros((heads, key_width, value_width), jnp.float32))

    def advance(carry, inputs):
        product, state = carry
        step_transit, step_offset, step_exposure, step_direct = inputs
        weight_in = jnp.einsum("hsd,hde->hse", step_exposure, product, precision=precise)
        local_out = (
            jnp.einsum("hsd,hde->hse", step_exposure, state, precision=precise) + step_direct
        )
        product = jnp.einsum("hij,hjk->hik", step_transit, product, precision=precise)
        state = jnp.einsum("hij,hjk->hik", step_transit, state, precision=precise) + step_offset
        return ((product, state), (weight_in, local_out))

    moved = (
        jnp.moveaxis(transit, 1, 0),
        jnp.moveaxis(offset, 1, 0),
        jnp.moveaxis(exposure, 1, 0),
        jnp.moveaxis(direct, 1, 0),
    )
    final_pair, outputs = lax.scan(advance, start, moved)
    return (final_pair[0], final_pair[1], outputs[0], outputs[1])


def per_device(
    residual,
    query_rows,
    key_rows,
    value_rows,
    log_decay,
    write_rate,
    output_weight,
    routes,
    route_gates,
    expert_up,
    expert_down,
):
    transit, offset, exposure, direct = block_terms(
        query_rows, key_rows, value_rows, log_decay, write_rate
    )
    product, state, weights_in, local_outs = shard_chain(transit, offset, exposure, direct)
    heads = product.shape[0]
    key_width = product.shape[1]
    value_width = state.shape[2]
    gathered_maps, gathered_offsets = (
        lax.all_gather(product, "seq", axis=0, tiled=True),
        lax.all_gather(state, "seq", axis=0, tiled=True),
    )
    shards = lax.axis_size("seq")
    gathered_maps = gathered_maps.reshape(shards, heads, key_width, key_width)
    gathered_offsets = gathered_offsets.reshape(shards, heads, key_width, value_width)
    position = lax.axis_index("seq")

    def absorb(index, current):
        return (
            jnp.einsum("hij,hjk->hik", gathered_maps[index], current, precision=precise)
            + gathered_offsets[index]
        )

    incoming = lax.fori_loop(
        0, position, absorb, jnp.zeros((heads, key_width, value_width), jnp.float32)
    )
    head_out = local_outs + jnp.einsum("nhsd,hde->nhse", weights_in, incoming, precision=precise)
    head_norm = head_out * lax.rsqrt(jnp.mean(head_out * head_out, axis=-1, keepdims=True) + 1e-06)
    head_norm = head_norm.astype(jnp.bfloat16)
    tokens = query_rows.shape[0]
    head_norm = jnp.transpose(head_norm, (0, 2, 1, 3)).reshape(tokens, heads * value_width)
    rows = residual.shape[0]
    attended = lax.psum_scatter(
        jnp.dot(head_norm, output_weight, preferred_element_type=jnp.float32),
        "expert",
        scatter_dimension=0,
        tiled=True,
    )
    mixed = (residual.astype(jnp.float32) + attended).astype(jnp.bfloat16)
    mixed_wide = mixed.astype(jnp.float32)
    expert_in = (
        mixed_wide * lax.rsqrt(jnp.mean(mixed_wide * mixed_wide, axis=-1, keepdims=True) + 1e-06)
    ).astype(jnp.bfloat16)
    seq_count = lax.axis_size("seq")
    lane_count = lax.axis_size("expert")
    experts = seq_count * lane_count
    chosen = routes.shape[1]
    capacity = 2 * rows * chosen // experts
    width = expert_in.shape[1]
    flat_routes = routes.reshape(-1)
    member = (flat_routes[:, None] == jnp.arange(experts, dtype=jnp.int32)[None, :]).astype(
        jnp.int32
    )
    earlier = jnp.sum((jnp.cumsum(member, axis=0) - member) * member, axis=1)
    slots = flat_routes * capacity + earlier
    sources = jnp.arange(rows * chosen, dtype=jnp.int32) // chosen
    outgoing = (
        jnp.zeros((experts * capacity, width), jnp.bfloat16).at[slots].set(expert_in[sources])
    )
    outgoing = outgoing.reshape(seq_count, lane_count, capacity, width)
    arrived = lax.all_to_all(
        lax.all_to_all(outgoing, "seq", split_axis=0, concat_axis=0, tiled=True),
        "expert",
        split_axis=1,
        concat_axis=1,
        tiled=True,
    ).reshape(-1, width)
    hidden_width = expert_down.shape[1]
    gate_up = jnp.dot(arrived, expert_up[0], preferred_element_type=jnp.float32)
    hidden = (jax.nn.silu(gate_up[:, :hidden_width]) * gate_up[:, hidden_width:]).astype(
        jnp.bfloat16
    )
    results = jnp.dot(hidden, expert_down[0], preferred_element_type=jnp.float32).astype(
        jnp.bfloat16
    )
    results = results.reshape(seq_count, lane_count, capacity, width)
    returned = lax.all_to_all(
        lax.all_to_all(results, "seq", split_axis=0, concat_axis=0, tiled=True),
        "expert",
        split_axis=1,
        concat_axis=1,
        tiled=True,
    ).reshape(experts * capacity, width)
    picked = returned[slots].astype(jnp.float32) * route_gates.reshape(-1)[:, None]
    combined = jnp.sum(picked.reshape(rows, chosen, width), axis=1)
    return (mixed_wide + combined).astype(jnp.bfloat16)


def solution(mesh):
    return jax.shard_map(
        per_device,
        mesh=mesh,
        in_specs=(
            P(("seq", "expert"), None),
            P("seq", "expert"),
            P("seq", "expert"),
            P("seq", "expert"),
            P("seq", "expert"),
            P("seq", "expert"),
            P("expert", None),
            P(("seq", "expert"), None),
            P(("seq", "expert"), None),
            P(("seq", "expert"), None, None),
            P(("seq", "expert"), None, None),
        ),
        out_specs=P(("seq", "expert"), None),
        check_vma=False,
    )
```

profile of v0, /device:TPU:0, one launch (start us, length us, event | category | flops | bytes accessed | tf_op | source)
XLA Modules:
  0.0 1433.2 jit_solution(17646969358656044937)
XLA Ops:
  6.6 1.6 convert_bitcast_fusion.1
  12.1 1.7 copy-done.11
  14.3 1.9 fusion.46
  17.8 9.6 add_bitcast_fusion
  27.3 316.0 %custom-call.3 = f32[8,8,1,64,64]{3,4,2,1,0:T(8,128)} custom-call(f32[8,8,1,64,64]{4,3,2,1,0:T(8,128)} %add_bitcast_fusion), custom_call_target="InvertDiagBlocksLowerTriangular" | custom-call | tf_op jit(solution)/shard_map/triangular_solve | solution.py:45
  348.6 5.3 fusion.42
  353.9 4.2 fusion.34
  358.1 3.6 fusion.61
  361.8 4.5 bitcast_subtract_fusion.1
  366.3 9.6 convolution_bitcast_fusion.1
  375.9 12.6 bitcast_subtract_fusion
  388.6 66.3 %while.28 = (s32[]{:T(128)}, f32[8,128,128]{2,1,0:T(8,128)S(1)}, f32[8,128,128]{2,1,0:T(8,128)S(1)}, f32[8,8,64,128]{3,2,0,1:T(8,128)}, f32[8,8,64,128]{3,2,0,1:...) while((s32[]{:T(128)}, f32[8,128,128]{2,1,0:T(8,128)S(1)}, ...), condition=%wide.region_4.5_spmd.clone, body=%wide.region_3.4_spmd.clone.sunk | while | flops 604438528 | bytes 8130168 | solution.py:92
  388.6 2.3 fusion.136
  390.9 1.8 convolution_add_fusion.6
  392.8 2.3 fusion.135
  395.1 1.7 fusion.134
  396.9 2.3 fusion.136
  399.2 1.8 convolution_add_fusion.6
  401.1 2.3 fusion.135
  403.4 1.7 fusion.134
  405.2 2.4 fusion.136
  407.5 1.8 convolution_add_fusion.6
  409.4 2.3 fusion.135
  411.7 1.7 fusion.134
  413.5 2.3 fusion.136
  415.8 1.8 convolution_add_fusion.6
  417.7 2.3 fusion.135
  420.0 1.7 fusion.134
  421.8 2.3 fusion.136
  424.1 1.8 convolution_add_fusion.6
  426.0 2.3 fusion.135
  428.3 1.7 fusion.134
  430.1 2.3 fusion.136
  432.4 1.8 convolution_add_fusion.6
  434.3 2.3 fusion.135
  436.6 1.7 fusion.134
  438.3 2.3 fusion.136
  440.7 1.8 convolution_add_fusion.6
  442.6 2.3 fusion.135
  444.9 1.7 fusion.134
  446.6 2.3 fusion.136
  449.0 1.8 convolution_add_fusion.6
  450.9 2.3 fusion.135
  453.1 1.7 fusion.134
  456.5 75.5 %all-gather.3.cloned.1.call-done = f32[64,128,128]{2,1,0:T(8,128)} async-done(((f32[8,128,128]{2,1,0:T(8,128)}), f32[64,128,128]{2,1,0:T(8,128)}) %all-gather.3.cloned.1.call-update) | async-done | bytes 4194320 | tf_op jit(solution)/shard_map/all_gather | solution.py:117
  531.9 73.8 %all-gather.5.cloned.1.call-done = f32[64,128,128]{2,1,0:T(8,128)} async-done(((f32[8,128,128]{2,1,0:T(8,128)}), f32[64,128,128]{2,1,0:T(8,128)}) %all-gather.5.cloned.1.call-update) | async-done | bytes 4194320 | tf_op jit(solution)/shard_map/all_gather | solution.py:118
  606.0 4.6 multiply_reduce_fusion
  612.1 6.6 fusion.76
  619.6 9.0 reduce-window.6
  629.4 49.0 %reduce-scatter.2.cloned.1.call-done = f32[128,2304]{1,0:T(8,128)} async-done(((f32[512,2304]{1,0:T(8,128)}), f32[128,2304]{1,0:T(8,128)}) %reduce-scatter.2.cloned.1.call-update) | async-done | bytes 1179664 | tf_op jit(solution)/shard_map/reduce_scatter | solution.py:140
  680.1 27.7 %scatter_custom_fusion = bf16[2048,2304]{1,0:T(8,128)(2,1)} fusion(s32[1024]{0:T(1024)S(1)} %bitcast.234, bf16[128,2304]{1,0:T(8,128)(2,1)S(1)} %fusion.73, s32[1024]{0:T(1024)S(1)} %broadcast_clamp_fusion.1, bf16[]{:T(256)} %constant.72.clone.1), kind=kCustom, calls=%fused_computation.39 | custom fusion | bytes 9437186 | tf_op jit(solution)/shard_map/scatter | solution.py:165
  707.8 211.8 %all_to_all.20 = bf16[8,4,64,2304]{3,2,1,0:T(8,128)(2,1)} all-to-all(bf16[8,4,64,2304]{3,2,1,0:T(8,128)(2,1)} %bitcast.217), channel_id=1, replica_groups=mesh['seq'=8,'expert'=4] {'seq'}, dimensions={0} | all-to-all | bytes 18874368 | tf_op jit(solution)/shard_map/all_to_all | solution.py:169
  919.6 8.3 copy.132
  927.9 112.3 %all_to_all.21 = bf16[8,4,64,2304]{3,2,0,1:T(8,128)(2,1)} all-to-all(bf16[8,4,64,2304]{3,2,0,1:T(8,128)(2,1)} %copy.132), channel_id=1, replica_groups=mesh['seq'=8,'expert'=4] {'expert'}, dimensions={1} | all-to-all | bytes 18874368 | tf_op jit(solution)/shard_map/all_to_all | solution.py:168
  1040.2 8.3 copy.133
  1048.5 13.9 fusion.28
  1062.4 5.9 convolution_convert_fusion
  1068.3 208.9 %all_to_all.22 = bf16[8,4,64,2304]{3,2,1,0:T(8,128)(2,1)} all-to-all(bf16[8,4,64,2304]{3,2,1,0:T(8,128)(2,1)S(1)} %bitcast.222), channel_id=1, replica_groups=mesh['seq'=8,'expert'=4] {'seq'}, dimensions={0} | all-to-all | bytes 18874368 | tf_op jit(solution)/shard_map/all_to_all | solution.py:185
  1277.2 8.3 copy.134
  1285.5 6.1 all-to-all-start.3
  1291.7 104.3 %all-to-all-done.3 = bf16[8,4,64,2304]{3,2,0,1:T(8,128)(2,1)} async-done(((bf16[8,4,64,2304]{3,2,0,1:T(8,128)(2,1)}), bf16[8,4,64,2304]{3,2,0,1:T(8,128)(2,1)}, u32[]{:S(2)}, u32[]{:S(2)}) %all-to-all-start.3) | async-done | bytes 9437216 | tf_op jit(solution)/shard_map/all_to_all | solution.py:184
  1396.0 8.3 copy.135
  1404.3 14.7 %gather_fusion = bf16[1024,2304]{1,0:T(8,128)(2,1)} fusion(bf16[2048,2304]{1,0:T(8,128)(2,1)} %bitcast.210, s32[1024]{0:T(1024)S(1)} %broadcast_clamp_fusion), kind=kCustom, calls=%fused_computation.1 | custom fusion | bytes 9441280 | tf_op jit(solution)/shard_map/gather | solution.py:191
  1419.0 6.6 fusion.27
  (105 shorter events, 19.3 us)
Async XLA Ops:
  6.5 1055.8 %copy-start = (bf16[1,512,2304]{2,1,0:T(8,128)(2,1)S(1)}, bf16[1,512,2304]{2,1,0:T(8,128)(2,1)}, u32[]{:S(2)}) copy-start(bf16[1,512,2304]{2,1,0:T(8,128)(2,1)} %param.25) | copy-start | bytes 7077892
  6.5 525.4 %all-gather.3.cloned.1.call-start = ((), (), s32[]{:S(2)}) async-start(), calls=%async_computation.5 | async-start | bytes 4718592 | tf_op jit(solution)/shard_map/all_gather | solution.py:117
  8.7 2.2 copy-start.3
  8.7 2.0 copy-start.12
  11.4 2.8 copy-start.6
  11.5 2.4 copy-start.11
  14.3 3.3 copy-start.14
  16.2 1.4 copy-start.1
  344.8 1.6 copy-start.2
  344.8 2.2 copy-start.4
  347.0 1.6 copy-start.7
  348.6 5.3 copy-start.10
  358.1 8.2 copy-start.5
  454.9 0.8 copy-start.8
  454.9 1.0 copy-start.9
  455.7 150.1 %all-gather.5.cloned.1.call-start = ((), (), s32[]{:S(2)}) async-start(), calls=%async_computation.6 | async-start | bytes 4718592 | tf_op jit(solution)/shard_map/all_gather | solution.py:118
  456.4 221.9 %reduce-scatter.2.cloned.1.call-start = ((), (), s32[]{:S(2)}) async-start(), calls=%async_computation.7 | async-start | bytes 5898240 | tf_op jit(solution)/shard_map/reduce_scatter | solution.py:140
  618.6 0.7 copy-start.15
  618.6 59.7 %copy-start.13 = (bf16[128,2304]{1,0:T(8,128)(2,1)S(1)}, bf16[128,2304]{1,0:T(8,128)(2,1)}, u32[]{:S(2)}) copy-start(bf16[128,2304]{1,0:T(8,128)(2,1)} %param.15) | copy-start | bytes 1769476
  1285.5 6.1 copy-start.16
  1285.5 110.5 %all-to-all-start.3 = ((bf16[8,4,64,2304]{3,2,0,1:T(8,128)(2,1)}), bf16[8,4,64,2304]{3,2,0,1:T(8,128)(2,1)}, u32[]{:S(2)}, u32[]{:S(2)}) async-start(bf16[8,4,64,2304]{3,2,0,1:T(8,128)(2,1)} %copy.134), calls=%async_computation.4 | async-start | bytes 18874368 | tf_op jit(solution)/shard_map/all_to_all | solution.py:184
Sparse Core Ops, SparseCore 0:
  455.8 76.0 all-gather.2
  534.1 71.6 all-gather.4
  618.8 59.5 reduce-scatter.1
where the time goes:
time: 1440 us; the launch traced here: 1430 us
  blocking collectives  533 us (37%)
  other arithmetic  343 us (24%)
  waiting for transfers between devices  303 us (21%)
  matrix products  146 us (10%)
  local copies, waits for them, and re-layouts  87.8 us (6%)
    another operation x2, other arithmetic, block_terms(): lax.linalg.triangular_solve(system, right_side, left_side=True, lower=Tru...  316 us
    all_to_all x1, blocking collectives, per_device(): lax.all_to_all(outgoing, 'seq', split_axis=0, concat_axis=0, tiled=True)  212 us
    all_to_all x1, blocking collectives, per_device(): lax.all_to_all(results, 'seq', split_axis=0, concat_axis=0, tiled=True)  209 us
    all_to_all x1, blocking collectives, per_device(): lax.all_to_all(lax.all_to_all(outgoing, 'seq', split_axis=0, concat_axis=...  112 us
    all_to_all x1, waiting for transfers between devices, per_device(): lax.all_to_all(lax.all_to_all(results, 'seq', split_axis=0, concat_axis=0...  104 us
    all_gather x1, waiting for transfers between devices, per_device(): lax.all_gather(product, 'seq', axis=0, tiled=True)  75.5 us
    all_gather x1, waiting for transfers between devices, per_device(): lax.all_gather(state, 'seq', axis=0, tiled=True)  73.8 us
    reduce_scatter x1, waiting for transfers between devices, per_device(): lax.psum_scatter(jnp.dot(head_norm, output_weight, preferred_element_type...  49 us
  transfers between devices with their start and end apart: 4, of which 4 were waited for; matrix products, arithmetic and copies ran while one was open for 1% of the time, Pallas kernels for 0%

commit v1 on v0

v1 whole, which is shorter than its diff:
```python
import jax
import jax.numpy as jnp
from jax import lax
from jax.sharding import PartitionSpec as P

BLOCK = 64


precise = lax.Precision.HIGH


def unit_rows(block):
    return block * lax.rsqrt(jnp.sum(block * block, axis=-1, keepdims=True) + 1e-06)


def head_blocks(array, heads):
    tokens = array.shape[0]
    width = array.shape[1] // heads
    shaped = array.reshape(tokens // BLOCK, BLOCK, heads, width)
    return jnp.transpose(shaped, (2, 0, 1, 3))


def unit_lower_inverse(lower_part):
    positions = jnp.arange(BLOCK)

    def off_diagonal(size):
        same = (positions[:, None] // (2 * size)) == (positions[None, :] // (2 * size))
        inner = (positions[:, None] // size) == (positions[None, :] // size)
        return jnp.where(same & ~inner, lower_part, 0.0)

    inverse = jnp.eye(BLOCK, dtype=jnp.float32) - off_diagonal(1)
    size = 2
    while size < BLOCK:
        part = jnp.einsum("hnst,hntu->hnsu", off_diagonal(size), inverse, precision=precise)
        inverse = inverse - jnp.einsum("hnst,hntu->hnsu", inverse, part, precision=precise)
        size *= 2
    return inverse


def block_terms(query_rows, key_rows, value_rows, log_decay, write_rate):
    heads = write_rate.shape[1]
    queries = unit_rows(head_blocks(query_rows.astype(jnp.float32), heads))
    keyed = unit_rows(head_blocks(key_rows.astype(jnp.float32), heads))
    values = head_blocks(value_rows.astype(jnp.float32), heads)
    rates = head_blocks(write_rate, heads)[..., 0]
    summed = jnp.cumsum(head_blocks(log_decay, heads), axis=2)
    middle = summed[:, :, BLOCK // 2 - 1 : BLOCK // 2, :]
    rising = jnp.exp(summed - middle)
    falling = jnp.exp(middle - summed)
    total_decay = summed[:, :, BLOCK - 1 :, :]
    key_down = keyed * falling
    scores = jnp.einsum("hnsd,hntd->hnst", keyed * rising, key_down, precision=precise)
    positions = jnp.arange(BLOCK)
    strict = positions[:, None] > positions[None, :]
    causal = positions[:, None] >= positions[None, :]
    lower_part = jnp.where(strict, scores * rates[..., None], 0.0)
    from_start = keyed * jnp.exp(summed)
    right_side = jnp.concatenate(
        [values * rates[..., None], from_start * rates[..., None]], axis=-1
    )
    inverse = unit_lower_inverse(lower_part)
    solved = jnp.einsum("hnst,hnte->hnse", inverse, right_side, precision=precise)
    value_width = values.shape[-1]
    fresh = solved[..., :value_width]
    carried = solved[..., value_width:]
    reach = jnp.where(
        causal, jnp.einsum("hnsd,hntd->hnst", queries * rising, key_down, precision=precise), 0.0
    )
    to_end = keyed * jnp.exp(total_decay - summed)
    key_width = keyed.shape[-1]
    transit = jnp.eye(key_width, dtype=jnp.float32) * jnp.exp(total_decay)[:, :, 0, :, None]
    transit = transit - jnp.einsum("hncd,hnce->hnde", to_end, carried, precision=precise)
    offset = jnp.einsum("hncd,hnce->hnde", to_end, fresh, precision=precise)
    exposure = queries * jnp.exp(summed) - jnp.einsum(
        "hnst,hntd->hnsd", reach, carried, precision=precise
    )
    direct = jnp.einsum("hnst,hnte->hnse", reach, fresh, precision=precise)
    return (transit, offset, exposure, direct)


def shard_chain(transit, offset, exposure, direct):
    heads, blocks, key_width = transit.shape[:3]
    value_width = offset.shape[-1]
    pair = jnp.concatenate(
        [
            jnp.broadcast_to(jnp.eye(key_width, dtype=jnp.float32), (heads, key_width, key_width)),
            jnp.zeros((heads, key_width, value_width), jnp.float32),
        ],
        axis=-1,
    )
    pairs = []
    for block in range(blocks):
        pairs.append(pair)
        pair = jnp.einsum("hij,hjk->hik", transit[:, block], pair, precision=precise)
        pair = pair.at[:, :, key_width:].add(offset[:, block])
    pairs = jnp.stack(pairs, axis=1)
    seen = jnp.einsum("hnsd,hnde->hnse", exposure, pairs, precision=precise)
    return (pair, seen[..., :key_width], seen[..., key_width:] + direct)


def incoming_states(pair):
    heads, key_width = pair.shape[:2]
    value_width = pair.shape[2] - key_width
    shards = lax.axis_size("seq")
    if heads == shards:
        mine = lax.all_to_all(pair, "seq", split_axis=0, concat_axis=0, tiled=True)
        state = jnp.zeros((key_width, value_width), jnp.float32)
        states = []
        for index in range(shards):
            states.append(state)
            if index < shards - 1:
                state = (
                    jnp.dot(mine[index, :, :key_width], state, precision=precise)
                    + mine[index, :, key_width:]
                )
        return lax.all_to_all(
            jnp.stack(states), "seq", split_axis=0, concat_axis=0, tiled=True
        )
    gathered = lax.all_gather(pair, "seq", axis=0, tiled=False)

    def absorb(index, current):
        return (
            jnp.einsum("hij,hjk->hik", gathered[index, :, :, :key_width], current, precision=precise)
            + gathered[index, :, :, key_width:]
        )

    return lax.fori_loop(
        0,
        lax.axis_index("seq"),
        absorb,
        jnp.zeros((heads, key_width, value_width), jnp.float32),
    )


def expert_rows(rows_in, expert_up, expert_down):
    hidden_width = expert_down.shape[0]
    gate_up = jnp.dot(rows_in, expert_up, preferred_element_type=jnp.float32)
    hidden = (jax.nn.silu(gate_up[:, :hidden_width]) * gate_up[:, hidden_width:]).astype(
        jnp.bfloat16
    )
    return jnp.dot(hidden, expert_down, preferred_element_type=jnp.float32).astype(jnp.bfloat16)


def routed_by_gather(expert_in, routes, route_gates, expert_up, expert_down):
    axes = ("seq", "expert")
    experts = lax.axis_size("seq") * lax.axis_size("expert")
    named = routes[:, :, None] == jnp.arange(experts, dtype=jnp.int32)[None, None, :]
    table = jnp.sum(jnp.where(named, route_gates[:, :, None], 0.0), axis=1)
    table = lax.all_gather(table, axes, axis=0, tiled=True)
    own = lax.axis_index("seq") * lax.axis_size("expert") + lax.axis_index("expert")
    gates = lax.dynamic_slice_in_dim(table, own, 1, axis=1)
    tokens = lax.all_gather(expert_in, axes, axis=0, tiled=True)
    results = expert_rows(tokens, expert_up[0], expert_down[0])
    share = (results.astype(jnp.float32) * gates).astype(jnp.bfloat16)
    return lax.psum_scatter(share, axes, scatter_dimension=0, tiled=True).astype(jnp.float32)


def routed_by_pairs(expert_in, routes, route_gates, expert_up, expert_down):
    seq_count = lax.axis_size("seq")
    lane_count = lax.axis_size("expert")
    experts = seq_count * lane_count
    chosen = routes.shape[1]
    rows = expert_in.shape[0]
    capacity = 2 * rows * chosen // experts
    width = expert_in.shape[1]
    flat_routes = routes.reshape(-1)
    member = (flat_routes[:, None] == jnp.arange(experts, dtype=jnp.int32)[None, :]).astype(
        jnp.int32
    )
    earlier = jnp.sum((jnp.cumsum(member, axis=0) - member) * member, axis=1)
    slots = flat_routes * capacity + earlier
    sources = jnp.arange(rows * chosen, dtype=jnp.int32) // chosen
    outgoing = (
        jnp.zeros((experts * capacity, width), jnp.bfloat16).at[slots].set(expert_in[sources])
    )
    outgoing = outgoing.reshape(seq_count, lane_count, capacity, width)
    arrived = lax.all_to_all(
        lax.all_to_all(outgoing, "seq", split_axis=0, concat_axis=0, tiled=True),
        "expert",
        split_axis=1,
        concat_axis=1,
        tiled=True,
    ).reshape(-1, width)
    results = expert_rows(arrived, expert_up[0], expert_down[0])
    results = results.reshape(seq_count, lane_count, capacity, width)
    returned = lax.all_to_all(
        lax.all_to_all(results, "seq", split_axis=0, concat_axis=0, tiled=True),
        "expert",
        split_axis=1,
        concat_axis=1,
        tiled=True,
    ).reshape(experts * capacity, width)
    picked = returned[slots].astype(jnp.float32) * route_gates.reshape(-1)[:, None]
    return jnp.sum(picked.reshape(rows, chosen, width), axis=1)

def per_device(
    residual,
    query_rows,
    key_rows,
    value_rows,
    log_decay,
    write_rate,
    output_weight,
    routes,
    route_gates,
    expert_up,
    expert_down,
):
    transit, offset, exposure, direct = block_terms(
        query_rows, key_rows, value_rows, log_decay, write_rate
    )
    pair, weights_in, local_outs = shard_chain(transit, offset, exposure, direct)
    heads = pair.shape[0]
    value_width = local_outs.shape[-1]
    incoming = incoming_states(pair)
    head_out = local_outs + jnp.einsum("hnsd,hde->hnse", weights_in, incoming, precision=precise)
    head_norm = head_out * lax.rsqrt(jnp.mean(head_out * head_out, axis=-1, keepdims=True) + 1e-06)
    head_norm = head_norm.astype(jnp.bfloat16)
    tokens = query_rows.shape[0]
    head_norm = jnp.transpose(head_norm, (1, 2, 0, 3)).reshape(tokens, heads * value_width)
    attended = lax.psum_scatter(
        jnp.dot(head_norm, output_weight, preferred_element_type=jnp.float32).astype(jnp.bfloat16),
        "expert",
        scatter_dimension=0,
        tiled=True,
    ).astype(jnp.float32)
    mixed = (residual.astype(jnp.float32) + attended).astype(jnp.bfloat16)
    mixed_wide = mixed.astype(jnp.float32)
    expert_in = (
        mixed_wide * lax.rsqrt(jnp.mean(mixed_wide * mixed_wide, axis=-1, keepdims=True) + 1e-06)
    ).astype(jnp.bfloat16)
    experts = lax.axis_size("seq") * lax.axis_size("expert")
    chosen = routes.shape[1]
    routed = routed_by_gather if experts <= 4 * chosen else routed_by_pairs
    combined = routed(expert_in, routes, route_gates, expert_up, expert_down)
    return (mixed_wide + combined).astype(jnp.bfloat16)


def solution(mesh):
    return jax.shard_map(
        per_device,
        mesh=mesh,
        in_specs=(
            P(("seq", "expert"), None),
            P("seq", "expert"),
            P("seq", "expert"),
            P("seq", "expert"),
            P("seq", "expert"),
            P("seq", "expert"),
            P("expert", None),
            P(("seq", "expert"), None),
            P(("seq", "expert"), None),
            P(("seq", "expert"), None, None),
            P(("seq", "expert"), None, None),
        ),
        out_specs=P(("seq", "expert"), None),
        check_vma=False,
    )
```

time: 1440 us -> 563 us (0.39)
  blocking collectives: 533 us -> 43.6 us
  other arithmetic: 343 us -> 13.9 us
  local copies, waits for them, and re-layouts: 87.8 us -> 24.2 us
  waiting for transfers between devices: 303 us -> 327 us
  matrix products: 146 us -> 123 us
    all_to_all x3 -> x0, blocking collectives: 533 us -> none  [the longest x1 212 us: per_device(): lax.all_to_all(outgoing, 'seq', split_axis=0, concat_axis=0, tiled=True)]
    another operation x7 -> x0, other arithmetic: 325 us -> none  [the longest x2 316 us: block_terms(): lax.linalg.triangular_solve(system, right_side, left_side=True, lower=Tru...]
    reduce_scatter x0 -> x1, waiting for transfers between devices: none -> 205 us  [routed_by_gather(): lax.psum_scatter(share, axes, scatter_dimension=0, tiled=True)]
    all_to_all x1 -> x2, waiting for transfers between devices: 104 us -> 7.27 us  [the longest x1 5.41 us: incoming_states(): mine = lax.all_to_all(pair, 'seq', split_axis=0, concat_axis=0, tiled=True)]
    all_gather x2 -> x1, waiting for transfers between devices: 149 us -> 82.4 us  [routed_by_gather(): tokens = lax.all_gather(expert_in, axes, axis=0, tiled=True)]
    all_gather x0 -> x1, blocking collectives: none -> 43.6 us  [routed_by_gather(): table = lax.all_gather(table, axes, axis=0, tiled=True)]
    all_to_all x4 -> x0, local copies, waits for them, and re-layouts: 33.2 us -> none  [the longest x1 8.31 us: per_device(): lax.all_to_all(outgoing, 'seq', split_axis=0, concat_axis=0, tiled=True)]
    scatter x1 -> x0, local copies, waits for them, and re-layouts: 27.7 us -> none  [per_device(): jnp.zeros((experts * capacity, width), jnp.bfloat16).at[slots]]
  transfers between devices with their start and end apart: 4 -> 5, of which waited for: 4 -> 5; matrix products, arithmetic and copies ran while one was open for 1% -> 5% of each run, Pallas kernels for 0% -> 0%
where the time goes in v1:
time: 563 us; the launch traced here: 558 us
  waiting for transfers between devices  327 us (58%)
  matrix products  123 us (22%)
  blocking collectives  43.6 us (8%)
  local copies, waits for them, and re-layouts  24.2 us (4%)
  other arithmetic  13.9 us (2%)
  between operations  13.9 us (2%)
  starting transfers between devices  12 us (2%)
    reduce_scatter x1, waiting for transfers between devices, routed_by_gather(): lax.psum_scatter(share, axes, scatter_dimension=0, tiled=True)  205 us
    all_gather x1, waiting for transfers between devices, routed_by_gather(): tokens = lax.all_gather(expert_in, axes, axis=0, tiled=True)  82.4 us
    all_gather x1, blocking collectives, routed_by_gather(): table = lax.all_gather(table, axes, axis=0, tiled=True)  43.6 us
    reduce_scatter x1, waiting for transfers between devices, per_device(): lax.psum_scatter(jnp.dot(head_norm, output_weight, preferred_element_type...  32.6 us
    dot_general x1, matrix products, expert_rows(): gate_up = jnp.dot(rows_in, expert_up, preferred_element_type=jnp.float32)  25.9 us
    unnamed x84, local copies, waits for them, and re-layouts  22.1 us
    dot_general x1, matrix products, expert_rows(): jnp.dot(hidden, expert_down, preferred_element_type=jnp.float32)  18.5 us
    dot_general x7, matrix products, incoming_states(): jnp.dot(mine[index, :, :key_width], state, precision=precise)  11.7 us
  transfers between devices with their start and end apart: 5, of which 5 were waited for; matrix products, arithmetic and copies ran while one was open for 5% of the time, Pallas kernels for 0%

profile of v1, /device:TPU:0, one launch (start us, length us, event | category | flops | bytes accessed | tf_op | source)
XLA Modules:
  0.0 558.2 jit_solution(5218241064593256219)
XLA Ops:
  6.6 2.2 copy.72
  8.8 1.4 fusion.16
  11.5 1.3 copy-done.5
  13.6 8.6 %multiply_select_fusion = f32[8,8,64,64]{3,2,1,0:T(8,128)S(1)} fusion(f32[8,8,64,128]{3,1,2,0:T(8,128)} %copy-done.1, f32[8,64,8,128]{3,2,1,0:T(8,128)} %bitcast.294, f32[8,8,64]{2,1,0:T(8,128)S(1)} %bitcast.306, f32[8,8,64]{2,1,0:T(8,128)S(1)} %add_rsqrt_fusion.1, f32[8,8,128]{2,1,0:T(8,128)S(1)} %get-tuple-element.103, ...), kind=kOutput, calls=%fused_computation.52 | convolution fusion | flops 204996608 | bytes 5312512 | tf_op jit(solution)/shard_map/hnsd,hntd->hnst/dot_general | solution.py:52
  22.3 1.3 fusion.30
  23.6 1.6 fusion.32
  25.2 1.3 fusion.28
  26.5 1.3 convolution_subtract_fusion.2
  27.8 1.3 fusion.26
  29.1 1.3 convolution_subtract_fusion.1
  30.4 1.3 fusion.24
  31.6 1.3 convolution_subtract_fusion
  32.9 1.4 fusion.22
  34.3 1.4 fusion.138
  36.5 1.1 copy-done.2
  37.6 0.6 copy-done.6
  38.2 1.4 bitcast_multiply_fusion
  39.6 2.4 fusion.6
  42.0 4.3 fusion.41
  46.3 5.4 multiply_subtract_fusion
  58.4 1.6 fusion.98
  60.0 1.9 fusion.97
  61.9 7.3 %all-to-all-start = ((f32[8,128,256]{2,1,0:T(8,128)}), f32[8,128,256]{2,1,0:T(8,128)}, u32[]{:S(2)}, u32[]{:S(2)}) async-start(f32[8,128,256]{2,1,0:T(8,128)} %fusion.97), calls=%async_computation | async-start | bytes 2097152 | tf_op jit(solution)/shard_map/all_to_all | solution.py:106
  69.2 2.2 fusion.67
  71.4 1.1 bitcast_dynamic-update-slice_fusion.6
  72.5 1.0 bitcast_dynamic-update-slice_fusion.5
  73.5 1.1 bitcast_dynamic-update-slice_fusion.4
  75.4 0.6 fusion.18
  76.0 0.6 constant_dynamic-update-slice_fusion
  76.7 0.7 copy-done.18
  77.3 1.1 bitcast_dynamic-update-slice_fusion.3
  78.4 1.1 bitcast_dynamic-update-slice_fusion.2
  79.5 1.0 bitcast_dynamic-update-slice_fusion.1
  80.6 0.9 copy-done.7
  81.5 4.2 fusion.36
  85.7 1.3 copy-done.12
  87.0 2.6 fusion.44
  89.6 5.4 all-to-all-done
  95.0 1.7 bitcast_dynamic-update-slice_fusion.12
  96.7 1.7 bitcast_dynamic-update-slice_fusion.11
  98.4 1.7 bitcast_dynamic-update-slice_fusion.10
  100.1 1.7 bitcast_dynamic-update-slice_fusion.9
  101.7 1.7 bitcast_dynamic-update-slice_fusion.8
  103.4 1.7 bitcast_dynamic-update-slice_fusion.7
  105.1 1.7 fusion.66
  106.8 4.2 all-to-all-start.1
  111.4 1.2 bitcast_dynamic-update-slice_fusion
  112.6 0.8 copy-done.4
  113.4 10.0 %fusion.1 = f32[8,8,64,256]{3,2,1,0:T(8,128)} fusion(f32[8,8,128,256]{3,2,0,1:T(8,128)} %bitcast_dynamic-update-slice_fusion, f32[8,8,64,128]{3,2,1,0:T(8,128)} %fusion.44, f32[8,64,8,128]{3,2,1,0:T(8,128)} %bitcast.301, f32[8,8,64,128]{3,1,2,0:T(8,128)S(1)} %copy-done.4, f32[8,8,64]{2,1,0:T(8,128)S(1)} %add_rsqrt_fusion.2), kind=kOutput, calls=%fused_computation.4 | convolution fusion | flops 806879232 | bytes 18890752 | tf_op jit(solution)/shard_map/hnsd,hnde->hnse/dot_general | solution.py:97
  123.3 1.9 all-to-all-done.1
  125.2 2.8 fusion.12
  128.2 4.2 multiply_reduce_fusion
  132.4 0.7 fusion.68
  133.1 0.7 copy.62
  133.9 3.8 convolution_convert_fusion.1
  137.8 32.6 %reduce-scatter.3.cloned.1.call-done = bf16[128,2304]{1,0:T(8,128)(2,1)} async-done(((bf16[512,2304]{1,0:T(8,128)(2,1)}), bf16[128,2304]{1,0:T(8,128)(2,1)}) %reduce-scatter.3.cloned.1.call-update) | async-done | bytes 589840 | tf_op jit(solution)/shard_map/reduce_scatter | solution.py:221
  170.4 1.3 fusion.62
  171.7 2.1 fusion.63
  173.9 43.6 %all_gather.7 = f32[4096,32]{0,1:T(8,128)S(1)} all-gather(f32[128,32]{0,1:T(8,128)S(1)} %select_reduce_fusion), channel_id=1, replica_groups=mesh['seq'=8,'expert'=4] {'seq','expert'}, dimensions={0}, use_global_device_ids=true | all-gather | bytes 540672 | tf_op jit(solution)/shard_map/all_gather | solution.py:149
  217.5 82.4 %all-gather.2.cloned.1.call-done = bf16[4096,2304]{1,0:T(8,128)(2,1)} async-done(((bf16[128,2304]{1,0:T(8,128)(2,1)}), bf16[4096,2304]{1,0:T(8,128)(2,1)}) %all-gather.2.cloned.1.call-update) | async-done | bytes 18874384 | tf_op jit(solution)/shard_map/all_gather | solution.py:152
  300.0 25.9 %fusion.3 = f32[4096,1024]{1,0:T(8,128)} fusion(bf16[4096,2304]{1,0:T(8,128)(2,1)} %all-gather.2.cloned.1.call-done, bf16[1,2304,1024]{2,1,0:T(8,128)(2,1)} %param.36), kind=kOutput, calls=%fused_computation.6 | convolution fusion | flops 19327352832 | bytes 40370176 | tf_op jit(solution)/shard_map/dot_general | solution.py:137
  325.9 18.5 %multiply_convert_fusion = bf16[4096,2304]{1,0:T(8,128)(2,1)} fusion(f32[4096]{0:T(1024)S(1)} %bitcast.308, f32[4096,1024]{1,0:T(8,128)} %fusion.3, bf16[1,512,2304]{2,1,0:T(8,128)(2,1)S(1)} %copy-done), kind=kOutput, calls=%fused_computation | convolution fusion | flops 9714008064 | bytes 38027264 | tf_op jit(solution)/shard_map/dot_general | solution.py:141
  344.4 205.0 %reduce-scatter.5.cloned.1.call-done = bf16[128,2304]{1,0:T(8,128)(2,1)} async-done(((bf16[4096,2304]{1,0:T(8,128)(2,1)}), bf16[128,2304]{1,0:T(8,128)(2,1)}) %reduce-scatter.5.cloned.1.call-update) | async-done | bytes 589840 | tf_op jit(solution)/shard_map/reduce_scatter | solution.py:155
  549.4 2.1 fusion.64
  (110 shorter events, 11.1 us)
Async XLA Ops:
  6.5 319.3 %copy-start = (bf16[1,512,2304]{2,1,0:T(8,128)(2,1)S(1)}, bf16[1,512,2304]{2,1,0:T(8,128)(2,1)}, u32[]{:S(2)}) copy-start(bf16[1,512,2304]{2,1,0:T(8,128)(2,1)} %param.37) | copy-start | bytes 7077892
  8.8 1.4 copy-start.28
  10.2 1.3 copy-start.1
  11.5 1.3 copy-start.5
  11.5 2.0 copy-start.31
  34.3 1.4 copy-start.29
  36.0 1.6 copy-start.2
  36.0 2.2 copy-start.6
  42.0 4.3 copy-start.8
  51.7 0.8 copy-start.27
  53.4 1.0 copy-start.13
  54.3 1.0 copy-start.15
  55.3 1.0 copy-start.17
  56.4 1.0 copy-start.19
  57.4 1.0 copy-start.21
  58.4 1.6 copy-start.23
  61.9 33.2 %all-to-all-start = ((f32[8,128,256]{2,1,0:T(8,128)}), f32[8,128,256]{2,1,0:T(8,128)}, u32[]{:S(2)}, u32[]{:S(2)}) async-start(f32[8,128,256]{2,1,0:T(8,128)} %fusion.97), calls=%async_computation | async-start | bytes 2097152 | tf_op jit(solution)/shard_map/all_to_all | solution.py:106
  69.2 3.3 copy-start.14
  71.4 2.1 copy-start.16
  72.5 2.1 copy-start.30
  75.3 5.2 copy-start.11
  75.3 2.0 copy-start.18
  75.3 3.1 copy-start.20
  77.3 2.2 copy-start.22
  78.4 2.1 copy-start.3
  78.4 3.1 copy-start.7
  81.5 5.5 copy-start.9
  85.7 1.3 copy-start.12
  89.6 21.8 %copy-start.24 = (f32[8,128,256]{2,1,0:T(8,128)S(1)}, f32[8,128,256]{2,1,0:T(8,128)}, u32[]{:S(2)}) copy-start(f32[8,128,256]{2,1,0:T(8,128)} %copy-done.23) | copy-start | bytes 3145732
  106.8 18.4 %all-to-all-start.1 = ((f32[8,128,128]{2,1,0:T(8,128)}), f32[8,128,128]{2,1,0:T(8,128)}, u32[]{:S(2)}, u32[]{:S(2)}) async-start(f32[8,128,128]{2,1,0:T(8,128)} %fusion.66), calls=%async_computation.1 | async-start | bytes 1048576 | tf_op jit(solution)/shard_map/all_to_all | solution.py:116
  110.9 59.4 %reduce-scatter.3.cloned.1.call-start = ((), (), s32[]{:S(2)}) async-start(), calls=%async_computation.4 | async-start | bytes 2949120 | tf_op jit(solution)/shard_map/reduce_scatter | solution.py:221
  111.4 2.0 copy-start.4
  125.2 3.0 copy-start.10
  125.2 8.6 %slice-start = ((s8[4718592]{0:T(1024)(128)(4,1)}), s8[4194304]{0:T(1024)(128)(4,1)S(1)}, s32[]{:S(2)}) async-start(s8[4718592]{0:T(1024)(128)(4,1)} %bitcast.309), calls=%async_computation.7 | async-start | bytes 8388608
  128.2 5.7 %slice-start.1 = ((s8[4718592]{0:T(1024)(128)(4,1)}), s8[524288]{0:T(1024)(128)(4,1)S(1)}, s32[]{:S(2)}) async-start(s8[4718592]{0:T(1024)(128)(4,1)} %bitcast.309), calls=%async_computation.8 | async-start | bytes 1048576
  137.7 32.7 %copy-start.25 = (bf16[128,2304]{1,0:T(8,128)(2,1)S(1)}, bf16[128,2304]{1,0:T(8,128)(2,1)}, u32[]{:S(2)}) copy-start(bf16[128,2304]{1,0:T(8,128)(2,1)} %param.27) | copy-start | bytes 1769476
  137.7 36.2 %copy-start.32 = (f32[128,8]{0,1:T(8,128)S(1)}, f32[128,8]{0,1:T(8,128)}, u32[]{:S(2)}) copy-start(f32[128,8]{0,1:T(8,128)} %param.35) | copy-start | bytes 12292
  137.7 36.2 %copy-start.33 = (s32[128,8]{0,1:T(8,128)S(1)}, s32[128,8]{0,1:T(8,128)}, u32[]{:S(2)}) copy-start(s32[128,8]{0,1:T(8,128)} %param.34) | copy-start | bytes 12292
  137.8 162.2 %all-gather.2.cloned.1.call-start = ((), (), s32[]{:S(2)}) async-start(), calls=%async_computation.5 | async-start | bytes 19464192 | tf_op jit(solution)/shard_map/all_gather | solution.py:152
  173.8 375.6 %reduce-scatter.5.cloned.1.call-start = ((), (), s32[]{:S(2)}) async-start(), calls=%async_computation.6 | async-start | bytes 19464192 | tf_op jit(solution)/shard_map/reduce_scatter | solution.py:155
  344.3 205.1 %copy-start.26 = (bf16[128,2304]{1,0:T(8,128)(2,1)S(1)}, bf16[128,2304]{1,0:T(8,128)(2,1)}, u32[]{:S(2)}) copy-start(bf16[128,2304]{1,0:T(8,128)(2,1)} %reduce-scatter.3.cloned.1.call-done) | copy-start | bytes 1769476
Sparse Core Ops, SparseCore 0:
  137.9 32.4 reduce-scatter.2
  174.0 125.9 all-gather.1
  344.5 204.8 reduce-scatter.4

commit v2 on v1

--- a/solution.py
+++ b/solution.py
@@ -4,6 +4,7 @@
 from jax.sharding import PartitionSpec as P
 
 BLOCK = 64
+PARTS = 2
 
 
 precise = lax.Precision.HIGH
@@ -141,18 +142,45 @@
     return jnp.dot(hidden, expert_down, preferred_element_type=jnp.float32).astype(jnp.bfloat16)
 
 
-def routed_by_gather(expert_in, routes, route_gates, expert_up, expert_down):
-    axes = ("seq", "expert")
-    experts = lax.axis_size("seq") * lax.axis_size("expert")
-    named = routes[:, :, None] == jnp.arange(experts, dtype=jnp.int32)[None, None, :]
-    table = jnp.sum(jnp.where(named, route_gates[:, :, None], 0.0), axis=1)
-    table = lax.all_gather(table, axes, axis=0, tiled=True)
-    own = lax.axis_index("seq") * lax.axis_size("expert") + lax.axis_index("expert")
-    gates = lax.dynamic_slice_in_dim(table, own, 1, axis=1)
-    tokens = lax.all_gather(expert_in, axes, axis=0, tiled=True)
-    results = expert_rows(tokens, expert_up[0], expert_down[0])
-    share = (results.astype(jnp.float32) * gates).astype(jnp.bfloat16)
-    return lax.psum_scatter(share, axes, scatter_dimension=0, tiled=True).astype(jnp.float32)
+def lane_weights(weights):
+    lanes = lax.axis_size("expert")
+    held = {0: weights}
+    step = lanes // 2
+    while step >= 1:
+        order = [(lane, lane ^ step) for lane in range(lanes)]
+        for m in list(held):
+            held[m ^ step] = tuple(lax.ppermute(part, "expert", order) for part in held[m])
+        step //= 2
+    return held
+
+
+def lane_gates(routes, route_gates):
+    shards, lanes = lax.axis_size("seq"), lax.axis_size("expert")
+    numbers = jnp.arange(shards * lanes, dtype=jnp.int32)
+    named = numbers[:, None, None] == routes.T[None, :, :]
+    table = jnp.sum(jnp.where(named, route_gates.T[None, :, :], 0.0), axis=1)
+    table = table.reshape(shards, lanes, routes.shape[0])
+    return lax.all_to_all(table, "seq", split_axis=0, concat_axis=0, tiled=True)
+
+
+def routed_by_gather(expert_in, gates, weights):
+    rows, width = expert_in.shape
+    shards = lax.axis_size("seq")
+    lane = lax.axis_index("expert")
+    part = rows // PARTS
+    results = []
+    for index in range(PARTS):
+        own = expert_in[index * part : (index + 1) * part]
+        tokens = lax.all_gather(own, "seq", axis=0, tiled=True)
+        total = jnp.zeros((shards * part, width), jnp.float32)
+        for m, (up, down) in weights.items():
+            gate = lax.dynamic_index_in_dim(gates, lane ^ m, axis=1, keepdims=False)
+            gate = gate[:, index * part : (index + 1) * part].reshape(-1, 1)
+            total += gate * expert_rows(tokens, up[0], down[0]).astype(jnp.float32)
+        results.append(
+            lax.psum_scatter(total.astype(jnp.bfloat16), "seq", scatter_dimension=0, tiled=True)
+        )
+    return jnp.concatenate(results, axis=0).astype(jnp.float32)
 
 
 def routed_by_pairs(expert_in, routes, route_gates, expert_up, expert_down):
@@ -206,6 +234,11 @@
     expert_up,
     expert_down,
 ):
+    experts = lax.axis_size("seq") * lax.axis_size("expert")
+    by_gather = experts <= 4 * routes.shape[1]
+    if by_gather:
+        gates = lane_gates(routes, route_gates)
+        weights = lane_weights((expert_up, expert_down))
     transit, offset, exposure, direct = block_terms(
         query_rows, key_rows, value_rows, log_decay, write_rate
     )
@@ -229,10 +262,10 @@
     expert_in = (
         mixed_wide * lax.rsqrt(jnp.mean(mixed_wide * mixed_wide, axis=-1, keepdims=True) + 1e-06)
     ).astype(jnp.bfloat16)
-    experts = lax.axis_size("seq") * lax.axis_size("expert")
-    chosen = routes.shape[1]
-    routed = routed_by_gather if experts <= 4 * chosen else routed_by_pairs
-    combined = routed(expert_in, routes, route_gates, expert_up, expert_down)
+    if by_gather:
+        combined = routed_by_gather(expert_in, gates, weights)
+    else:
+        combined = routed_by_pairs(expert_in, routes, route_gates, expert_up, expert_down)
     return (mixed_wide + combined).astype(jnp.bfloat16)
 
 

time: 563 us -> 509 us (0.904)
  blocking collectives: 43.6 us -> 0 us
  waiting for transfers between devices: 327 us -> 295 us
  matrix products: 123 us -> 140 us
  starting transfers between devices: 12 us -> 18.2 us
    ppermute x0 -> x6, waiting for transfers between devices: none -> 105 us  [lane_weights(): lax.ppermute(part, 'expert', order)]
    reduce_scatter x1 -> x2, waiting for transfers between devices: 205 us -> 111 us  [routed_by_gather(): lax.psum_scatter(total.astype(jnp.bfloat16), 'seq', scatter_dimension=0,...]
    all_gather x1 -> x2, waiting for transfers between devices: 82.4 us -> 20.1 us  [routed_by_gather(): tokens = lax.all_gather(own, 'seq', axis=0, tiled=True)]
    all_gather x1 -> x0, blocking collectives: 43.6 us -> none  [routed_by_gather(): table = lax.all_gather(table, axes, axis=0, tiled=True)]
    dot_general x1 -> x8, matrix products: 25.9 us -> 37.3 us  [expert_rows(): gate_up = jnp.dot(rows_in, expert_up, preferred_element_type=jnp.float32)]
    reduce_scatter x1, waiting for transfers between devices: 32.6 us -> 43.3 us  [per_device(): lax.psum_scatter(jnp.dot(head_norm, output_weight, preferred_element_type...]
    dot_general x1 -> x8, matrix products: 18.5 us -> 26.5 us  [expert_rows(): jnp.dot(hidden, expert_down, preferred_element_type=jnp.float32)]
    all_to_all x0 -> x1, waiting for transfers between devices: none -> 6.24 us  [lane_gates(): return lax.all_to_all(table, 'seq', split_axis=0, concat_axis=0, tiled=True)]
  transfers between devices with their start and end apart: 5 -> 14, of which waited for: 5 -> 9; matrix products, arithmetic and copies ran while one was open for 5% -> 19% of each run, Pallas kernels for 0% -> 0%
where the time goes in v2:
time: 509 us; the launch traced here: 504 us
  waiting for transfers between devices  295 us (58%)
  matrix products  140 us (28%)
  local copies, waits for them, and re-layouts  23.7 us (5%)
  starting transfers between devices  18.2 us (4%)
  between operations  14.2 us (3%)
  other arithmetic  13.8 us (3%)
    reduce_scatter x2, waiting for transfers between devices, routed_by_gather(): lax.psum_scatter(total.astype(jnp.bfloat16), 'seq', scatter_dimension=0,...  111 us
    ppermute x6, waiting for transfers between devices, lane_weights(): lax.ppermute(part, 'expert', order)  105 us
    reduce_scatter x1, waiting for transfers between devices, per_device(): lax.psum_scatter(jnp.dot(head_norm, output_weight, preferred_element_type...  43.3 us
    dot_general x8, matrix products, expert_rows(): gate_up = jnp.dot(rows_in, expert_up, preferred_element_type=jnp.float32)  37.3 us
    dot_general x8, matrix products, expert_rows(): jnp.dot(hidden, expert_down, preferred_element_type=jnp.float32)  26.5 us
    all_gather x2, waiting for transfers between devices, routed_by_gather(): tokens = lax.all_gather(own, 'seq', axis=0, tiled=True)  20.1 us
    unnamed x82, local copies, waits for them, and re-layouts  19.9 us
    dot_general x7, matrix products, incoming_states(): jnp.dot(mine[index, :, :key_width], state, precision=precise)  11.7 us
  transfers between devices with their start and end apart: 14, of which 9 were waited for; matrix products, arithmetic and copies ran while one was open for 19% of the time, Pallas kernels for 0%

profile of v2, /device:TPU:0, one launch (start us, length us, event | category | flops | bytes accessed | tf_op | source)
XLA Modules:
  0.0 504.5 jit_solution(1939542825738846085)
XLA Ops:
  6.6 2.1 copy.68
  8.7 1.4 fusion.34
  10.8 1.3 copy-done
  12.8 6.1 %multiply_select_fusion = f32[8,8,64,64]{3,2,1,0:T(8,128)S(1)} fusion(f32[8,8,64,128]{3,1,2,0:T(8,128)S(1)} %fusion.34, f32[8,64,8,128]{3,2,1,0:T(8,128)} %bitcast.341, f32[8,8,64]{2,1,0:T(8,128)S(1)} %bitcast.353, f32[8,8,64]{2,1,0:T(8,128)S(1)} %add_rsqrt_fusion.1, f32[8,8,128]{2,1,0:T(8,128)S(1)} %get-tuple-element.103, ...), kind=kOutput, calls=%fused_computation.78 | convolution fusion | flops 204996608 | bytes 5312512 | tf_op jit(solution)/shard_map/hnsd,hntd->hnst/dot_general | solution.py:53
  19.1 1.3 fusion.48
  20.3 1.6 fusion.50
  23.2 1.3 convolution_subtract_fusion.2
  25.8 1.3 convolution_subtract_fusion.1
  28.3 1.3 convolution_subtract_fusion
  29.6 1.4 fusion.40
  31.0 1.4 fusion.192
  34.3 1.4 bitcast_multiply_fusion
  35.7 2.4 fusion.18
  38.1 4.3 fusion.59
  42.5 5.5 %multiply_subtract_fusion = f32[8,8,128,128]{3,2,1,0:T(8,128)S(1)} fusion(f32[8,8,128]{2,1,0:T(8,128)S(1)} %get-tuple-element.102, f32[128,128]{1,0:T(8,128)S(1)} %fusion.162, f32[8,8,64,256]{3,2,1,0:T(8,128)S(1)} %fusion.18, f32[8,8,64,128]{3,1,2,0:T(8,128)S(1)} %fusion.34, f32[8,64,8,128]{3,2,1,0:T(8,128)S(1)} %bitcast.344, ...), kind=kOutput, calls=%fused_computation.33 | convolution fusion | flops 406323200 | bytes 10649600 | tf_op jit(solution)/shard_map/hncd,hnce->hnde/dot_general | solution.py:73
  54.6 1.6 fusion.132
  56.2 1.9 fusion.131
  58.2 7.3 %all-to-all-start = ((f32[8,128,256]{2,1,0:T(8,128)}), f32[8,128,256]{2,1,0:T(8,128)}, u32[]{:S(2)}, u32[]{:S(2)}) async-start(f32[8,128,256]{2,1,0:T(8,128)} %fusion.131), calls=%async_computation | async-start | bytes 2097152 | tf_op jit(solution)/shard_map/all_to_all | solution.py:107
  65.4 2.2 fusion.85
  76.8 4.2 fusion.54
  81.0 1.3 copy-done.8
  82.4 2.6 fusion.62
  84.9 6.4 %all-to-all-done = f32[8,128,256]{2,1,0:T(8,128)} async-done(((f32[8,128,256]{2,1,0:T(8,128)}), f32[8,128,256]{2,1,0:T(8,128)}, u32[]{:S(2)}, u32[]{:S(2)}) %all-to-all-start) | async-done | bytes 1048608 | tf_op jit(solution)/shard_map/all_to_all | solution.py:107
  91.3 1.7 bitcast_dynamic-update-slice_fusion.12
  93.0 1.7 bitcast_dynamic-update-slice_fusion.11
  94.6 1.7 bitcast_dynamic-update-slice_fusion.10
  96.3 1.7 bitcast_dynamic-update-slice_fusion.9
  98.0 1.7 bitcast_dynamic-update-slice_fusion.8
  99.7 1.7 bitcast_dynamic-update-slice_fusion.7
  101.4 1.7 fusion.84
  103.0 4.2 all-to-all-start.1
  109.6 9.3 %fusion = f32[8,8,64,256]{3,2,1,0:T(8,128)} fusion(f32[8,8,128,256]{3,2,0,1:T(8,128)} %bitcast_dynamic-update-slice_fusion, f32[8,8,64,128]{3,2,1,0:T(8,128)} %fusion.62, f32[8,64,8,128]{3,2,1,0:T(8,128)S(1)} %bitcast.348, f32[8,8,64,128]{3,1,2,0:T(8,128)S(1)} %fusion.34, f32[8,8,64]{2,1,0:T(8,128)S(1)} %add_rsqrt_fusion.2), kind=kOutput, calls=%fused_computation | convolution fusion | flops 806879232 | bytes 18890752 | tf_op jit(solution)/shard_map/hnsd,hnde->hnse/dot_general | solution.py:98
  119.0 2.5 all-to-all-done.1
  121.5 2.8 fusion.30
  124.4 4.2 multiply_reduce_fusion
  130.1 3.8 convolution_convert_fusion.8
  134.0 1.6 collective-permute-start
  135.6 43.3 %reduce-scatter.4.cloned.1.call-done = bf16[128,2304]{1,0:T(8,128)(2,1)} async-done(((bf16[512,2304]{1,0:T(8,128)(2,1)}), bf16[128,2304]{1,0:T(8,128)(2,1)}) %reduce-scatter.4.cloned.1.call-update) | async-done | bytes 589840 | tf_op jit(solution)/shard_map/reduce_scatter | solution.py:254
  178.9 1.3 fusion.80
  180.3 1.3 fusion.81
  182.8 69.0 %collective-permute-done = bf16[1,2304,1024]{2,1,0:T(8,128)(2,1)} collective-permute-done((bf16[1,2304,1024]{2,1,0:T(8,128)(2,1)}, bf16[1,2304,1024]{2,1,0:T(8,128)(2,1)}, u32[]{:S(2)}, u32[]{:S(2)}) %collective-permute-start) | collective-permute-done | bytes 4718624 | tf_op jit(solution)/shard_map/ppermute | solution.py:152
  252.4 3.6 all-to-all-start.2
  256.3 6.2 %all-to-all-done.2 = f32[8,4,128]{2,1,0:T(4,128)S(1)} async-done(((f32[8,4,128]{2,1,0:T(4,128)}), f32[8,4,128]{2,1,0:T(4,128)S(1)}, u32[]{:S(2)}, u32[]{:S(2)}) %all-to-all-start.2) | async-done | bytes 16416 | tf_op jit(solution)/shard_map/all_to_all | solution.py:163
  263.5 36.2 %collective-permute-done.1 = bf16[1,512,2304]{2,1,0:T(8,128)(2,1)} collective-permute-done((bf16[1,512,2304]{2,1,0:T(8,128)(2,1)S(1)}, bf16[1,512,2304]{2,1,0:T(8,128)(2,1)}, u32[]{:S(2)}, u32[]{:S(2)}) %collective-permute-start.1) | collective-permute-done | bytes 2359328 | tf_op jit(solution)/shard_map/ppermute | solution.py:152
  299.9 5.2 %fusion.16 = f32[512,1024]{1,0:T(8,128)S(1)} fusion(bf16[512,2304]{1,0:T(8,128)(2,1)} %all-gather.3.cloned.1.call-done, bf16[1,2304,1024]{2,1,0:T(8,128)(2,1)} %param.36), kind=kOutput, calls=%fused_computation.16 | convolution fusion | flops 2415919104 | bytes 9175040 | tf_op jit(solution)/shard_map/dot_general | solution.py:138
  305.1 1.6 convolution_convert_fusion.7
  306.8 4.5 fusion.12
  311.4 3.2 convolution_convert_fusion.6
  314.6 4.5 fusion.8
  319.1 3.2 convolution_convert_fusion.5
  322.3 4.5 fusion.4
  326.8 5.4 %add_convert_fusion.1 = bf16[512,2304]{1,0:T(8,128)(2,1)} fusion(bf16[512,2304]{1,0:T(8,128)(2,1)S(1)} %convolution_convert_fusion.5, bf16[512,2304]{1,0:T(8,128)(2,1)S(1)} %convolution_convert_fusion.6, bf16[512,2304]{1,0:T(8,128)(2,1)S(1)} %convolution_convert_fusion.7, bf16[1,512,2304]{2,1,0:T(8,128)(2,1)} %collective-permute-done.5, f32[512]{0:T(512)S(1)} %mul.273, ...), kind=kOutput, calls=%fused_computation.19 | convolution fusion | flops 1224867840 | bytes 13901824 | tf_op jit(solution)/shard_map/dot_general | solution.py:142
  332.5 20.1 %all-gather.5.cloned.1.call-done = bf16[512,2304]{1,0:T(8,128)(2,1)} async-done(((bf16[64,2304]{1,0:T(8,128)(2,1)}), bf16[512,2304]{1,0:T(8,128)(2,1)}) %all-gather.5.cloned.1.call-update) | async-done | bytes 2359312 | tf_op jit(solution)/shard_map/all_gather | solution.py:174
  352.6 5.2 %fusion.14 = f32[512,1024]{1,0:T(8,128)S(1)} fusion(bf16[512,2304]{1,0:T(8,128)(2,1)} %all-gather.5.cloned.1.call-done, bf16[1,2304,1024]{2,1,0:T(8,128)(2,1)} %param.36), kind=kOutput, calls=%fused_computation.14 | convolution fusion | flops 2415919104 | bytes 9175040 | tf_op jit(solution)/shard_map/dot_general | solution.py:138
  357.8 1.6 convolution_convert_fusion.3
  359.4 4.5 fusion.10
  363.9 3.2 convolution_convert_fusion.2
  367.1 4.5 fusion.6
  371.6 3.3 convolution_convert_fusion.1
  374.8 4.5 fusion.2
  379.4 5.1 %add_convert_fusion = bf16[512,2304]{1,0:T(8,128)(2,1)} fusion(bf16[512,2304]{1,0:T(8,128)(2,1)S(1)} %convolution_convert_fusion.1, bf16[512,2304]{1,0:T(8,128)(2,1)S(1)} %convolution_convert_fusion.2, bf16[512,2304]{1,0:T(8,128)(2,1)S(1)} %convolution_convert_fusion.3, bf16[1,512,2304]{2,1,0:T(8,128)(2,1)} %collective-permute-done.5, f32[512]{0:T(512)S(1)} %mul.293, ...), kind=kOutput, calls=%fused_computation.18 | convolution fusion | flops 1224867840 | bytes 13901824 | tf_op jit(solution)/shard_map/dot_general | solution.py:142
  384.5 39.4 %reduce-scatter.6.cloned.1.call-done = bf16[64,2304]{1,0:T(8,128)(2,1)} async-done(((bf16[512,2304]{1,0:T(8,128)(2,1)}), bf16[64,2304]{1,0:T(8,128)(2,1)}) %reduce-scatter.6.cloned.1.call-update) | async-done | bytes 294928 | tf_op jit(solution)/shard_map/reduce_scatter | solution.py:181
  423.9 71.8 %reduce-scatter.8.cloned.1.call-done = bf16[64,2304]{1,0:T(8,128)(2,1)} async-done(((bf16[512,2304]{1,0:T(8,128)(2,1)}), bf16[64,2304]{1,0:T(8,128)(2,1)}) %reduce-scatter.8.cloned.1.call-update) | async-done | bytes 294928 | tf_op jit(solution)/shard_map/reduce_scatter | solution.py:181
  495.6 2.1 fusion.82
  (154 shorter events, 30.8 us)
Async XLA Ops:
  8.7 1.4 copy-start.24
  10.8 1.3 copy-start
  10.8 1.9 copy-start.27
  31.0 1.4 copy-start.25
  32.7 1.6 copy-start.1
  38.1 4.3 copy-start.3
  48.0 0.8 copy-start.23
  49.7 1.0 copy-start.9
  50.7 1.0 copy-start.11
  51.7 1.0 copy-start.13
  52.6 1.0 copy-start.15
  53.6 1.0 copy-start.17
  54.6 1.6 copy-start.19
  58.2 33.2 %all-to-all-start = ((f32[8,128,256]{2,1,0:T(8,128)}), f32[8,128,256]{2,1,0:T(8,128)}, u32[]{:S(2)}, u32[]{:S(2)}) async-start(f32[8,128,256]{2,1,0:T(8,128)} %fusion.131), calls=%async_computation | async-start | bytes 2097152 | tf_op jit(solution)/shard_map/all_to_all | solution.py:107
  65.4 3.3 copy-start.10
  67.7 2.2 copy-start.12
  68.8 2.1 copy-start.26
  71.6 5.2 %copy-start.6 = (f32[64,8,8,128]{3,2,1,0:T(8,128)}, f32[64,8,8,128]{3,2,1,0:T(8,128)S(1)}, u32[]{:S(2)}) copy-start(f32[64,8,8,128]{3,2,1,0:T(8,128)S(1)} %copy.67) | copy-start | bytes 6291460
  71.6 2.0 copy-start.14
  71.6 3.1 copy-start.16
  73.6 2.1 copy-start.18
  74.7 2.1 copy-start.2
  76.8 5.6 %copy-start.4 = (f32[8,8,64,256]{3,2,1,0:T(8,128)S(1)}, f32[8,8,64,256]{3,2,1,0:T(8,128)}, u32[]{:S(2)}) copy-start(f32[8,8,64,256]{3,2,1,0:T(8,128)} %copy-done.3) | copy-start | bytes 12582916
  81.0 1.4 copy-start.8
  84.9 22.7 %copy-start.20 = (f32[8,128,256]{2,1,0:T(8,128)S(1)}, f32[8,128,256]{2,1,0:T(8,128)}, u32[]{:S(2)}) copy-start(f32[8,128,256]{2,1,0:T(8,128)} %copy-done.19) | copy-start | bytes 3145732
  103.0 18.4 %all-to-all-start.1 = ((f32[8,128,128]{2,1,0:T(8,128)}), f32[8,128,128]{2,1,0:T(8,128)}, u32[]{:S(2)}, u32[]{:S(2)}) async-start(f32[8,128,128]{2,1,0:T(8,128)} %fusion.84), calls=%async_computation.1 | async-start | bytes 1048576 | tf_op jit(solution)/shard_map/all_to_all | solution.py:117
  107.2 71.7 %reduce-scatter.4.cloned.1.call-start = ((), (), s32[]{:S(2)}) async-start(), calls=%async_computation.6 | async-start | bytes 2949120 | tf_op jit(solution)/shard_map/reduce_scatter | solution.py:254
  107.7 2.0 copy-start.7
  121.5 3.0 copy-start.5
  121.5 8.6 %slice-start = ((s8[4718592]{0:T(1024)(128)(4,1)}), s8[4194304]{0:T(1024)(128)(4,1)S(1)}, s32[]{:S(2)}) async-start(s8[4718592]{0:T(1024)(128)(4,1)} %bitcast.361), calls=%async_computation.11 | async-start | bytes 8388608
  124.4 5.6 %slice-start.1 = ((s8[4718592]{0:T(1024)(128)(4,1)}), s8[524288]{0:T(1024)(128)(4,1)S(1)}, s32[]{:S(2)}) async-start(s8[4718592]{0:T(1024)(128)(4,1)} %bitcast.361), calls=%async_computation.12 | async-start | bytes 1048576
  133.9 45.0 %copy-start.21 = (bf16[128,2304]{1,0:T(8,128)(2,1)S(1)}, bf16[128,2304]{1,0:T(8,128)(2,1)}, u32[]{:S(2)}) copy-start(bf16[128,2304]{1,0:T(8,128)(2,1)} %param.27) | copy-start | bytes 1769476
  133.9 48.5 %copy-start.30 = (bf16[1,512,2304]{2,1,0:T(8,128)(2,1)S(1)}, bf16[1,512,2304]{2,1,0:T(8,128)(2,1)}, u32[]{:S(2)}) copy-start(bf16[1,512,2304]{2,1,0:T(8,128)(2,1)} %param.37) | copy-start | bytes 7077892
  133.9 117.8 %copy-start.28 = (f32[128,8]{0,1:T(8,128)S(1)}, f32[128,8]{0,1:T(8,128)}, u32[]{:S(2)}) copy-start(f32[128,8]{0,1:T(8,128)} %param.35) | copy-start | bytes 12292
  133.9 117.8 %copy-start.29 = (s32[128,8]{0,1:T(8,128)S(1)}, s32[128,8]{0,1:T(8,128)}, u32[]{:S(2)}) copy-start(s32[128,8]{0,1:T(8,128)} %param.34) | copy-start | bytes 12292
  134.0 166.0 %all-gather.3.cloned.1.call-start = ((), (), s32[]{:S(2)}) async-start(), calls=%async_computation.7 | async-start | bytes 2654208 | tf_op jit(solution)/shard_map/all_gather | solution.py:174
  134.0 117.8 %collective-permute-start = (bf16[1,2304,1024]{2,1,0:T(8,128)(2,1)}, bf16[1,2304,1024]{2,1,0:T(8,128)(2,1)}, u32[]{:S(2)}, u32[]{:S(2)}) collective-permute-start(bf16[1,2304,1024]{2,1,0:T(8,128)(2,1)} %param.36), channel_id=1, source_target_pairs={{0,2},{1,3},{2,0},{3,1},{4,6},{5,7},{6,4},{7,5},{8,10},{9,11},{10,... | collective-permute-start | bytes 14155784 | tf_op jit(solution)/shard_map/ppermute | solution.py:152
  182.4 117.2 %collective-permute-start.1 = (bf16[1,512,2304]{2,1,0:T(8,128)(2,1)S(1)}, bf16[1,512,2304]{2,1,0:T(8,128)(2,1)}, u32[]{:S(2)}, u32[]{:S(2)}) collective-permute-start(bf16[1,512,2304]{2,1,0:T(8,128)(2,1)S(1)} %copy-done.30), channel_id=1, source_target_pairs={{0,2},{1,3},{2,0},{3,1},{4,6},{5,7},{6,4},{7,5},{8,10},{9,11},{10,... | collective-permute-start | bytes 7077896 | tf_op jit(solution)/shard_map/ppermute | solution.py:152
  182.8 131.8 %collective-permute-start.2 = (bf16[1,2304,1024]{2,1,0:T(8,128)(2,1)}, bf16[1,2304,1024]{2,1,0:T(8,128)(2,1)}, u32[]{:S(2)}, u32[]{:S(2)}) collective-permute-start(bf16[1,2304,1024]{2,1,0:T(8,128)(2,1)} %param.36), channel_id=1, source_target_pairs={{0,1},{1,0},{2,3},{3,2},{4,5},{5,4},{6,7},{7,6},{8,9},{9,8},{10,11... | collective-permute-start | bytes 14155784 | tf_op jit(solution)/shard_map/ppermute | solution.py:152
  251.8 70.6 %collective-permute-start.4 = (bf16[1,2304,1024]{2,1,0:T(8,128)(2,1)}, bf16[1,2304,1024]{2,1,0:T(8,128)(2,1)}, u32[]{:S(2)}, u32[]{:S(2)}) collective-permute-start(bf16[1,2304,1024]{2,1,0:T(8,128)(2,1)} %collective-permute-done), channel_id=1, source_target_pairs={{0,1},{1,0},{2,3},{3,2},{4,5},{5,4},{6,7},{7,6},{8,9},{9,8},{10,11... | collective-permute-start | bytes 14155784 | tf_op jit(solution)/shard_map/ppermute | solution.py:152
  252.4 10.1 %all-to-all-start.2 = ((f32[8,4,128]{2,1,0:T(4,128)}), f32[8,4,128]{2,1,0:T(4,128)S(1)}, u32[]{:S(2)}, u32[]{:S(2)}) async-start(f32[8,4,128]{2,1,0:T(4,128)} %bitcast.60), calls=%async_computation.3 | async-start | bytes 32768 | tf_op jit(solution)/shard_map/all_to_all | solution.py:163
  256.0 96.6 %all-gather.5.cloned.1.call-start = ((), (), s32[]{:S(2)}) async-start(), calls=%async_computation.9 | async-start | bytes 2654208 | tf_op jit(solution)/shard_map/all_gather | solution.py:174
  256.0 63.0 %collective-permute-start.3 = (bf16[1,512,2304]{2,1,0:T(8,128)(2,1)S(1)}, bf16[1,512,2304]{2,1,0:T(8,128)(2,1)}, u32[]{:S(2)}, u32[]{:S(2)}) collective-permute-start(bf16[1,512,2304]{2,1,0:T(8,128)(2,1)S(1)} %copy-done.30), channel_id=1, source_target_pairs={{0,1},{1,0},{2,3},{3,2},{4,5},{5,4},{6,7},{7,6},{8,9},{9,8},{10,11... | collective-permute-start | bytes 7077896 | tf_op jit(solution)/shard_map/ppermute | solution.py:152
  299.7 27.1 %collective-permute-start.5 = (bf16[1,512,2304]{2,1,0:T(8,128)(2,1)}, bf16[1,512,2304]{2,1,0:T(8,128)(2,1)}, u32[]{:S(2)}, u32[]{:S(2)}) collective-permute-start(bf16[1,512,2304]{2,1,0:T(8,128)(2,1)} %collective-permute-done.1), channel_id=1, source_target_pairs={{0,1},{1,0},{2,3},{3,2},{4,5},{5,4},{6,7},{7,6},{8,9},{9,8},{10,11... | collective-permute-start | bytes 7077896 | tf_op jit(solution)/shard_map/ppermute | solution.py:152
  299.7 124.2 %reduce-scatter.6.cloned.1.call-start = ((), (), s32[]{:S(2)}) async-start(), calls=%async_computation.8 | async-start | bytes 2654208 | tf_op jit(solution)/shard_map/reduce_scatter | solution.py:181
  305.1 1.7 copy-start.31
  332.2 163.4 %reduce-scatter.8.cloned.1.call-start = ((), (), s32[]{:S(2)}) async-start(), calls=%async_computation.10 | async-start | bytes 2654208 | tf_op jit(solution)/shard_map/reduce_scatter | solution.py:181
  357.7 1.7 copy-start.32
  384.4 111.2 %copy-start.22 = (bf16[128,2304]{1,0:T(8,128)(2,1)S(1)}, bf16[128,2304]{1,0:T(8,128)(2,1)}, u32[]{:S(2)}) copy-start(bf16[128,2304]{1,0:T(8,128)(2,1)} %reduce-scatter.4.cloned.1.call-done) | copy-start | bytes 1769476
Sparse Core Ops, SparseCore 0:
  134.0 44.8 reduce-scatter.3
  182.5 52.0 all-gather.2
  299.8 52.7 all-gather.4
  356.3 67.5 reduce-scatter.5
  427.6 67.9 reduce-scatter.7

commit v3 on v2

--- a/solution.py
+++ b/solution.py
@@ -142,16 +142,76 @@
     return jnp.dot(hidden, expert_down, preferred_element_type=jnp.float32).astype(jnp.bfloat16)
 
 
-def lane_weights(weights):
+def tie(value, moved):
+    return lax.optimization_barrier((value, moved))
+
+
+def far_lane(part):
     lanes = lax.axis_size("expert")
-    held = {0: weights}
-    step = lanes // 2
+    return lax.ppermute(part, "expert", [(lane, lane ^ (lanes // 2)) for lane in range(lanes)])
+
+
+def lane_weights(held):
+    lanes = lax.axis_size("expert")
+    step = lanes // 4
     while step >= 1:
         order = [(lane, lane ^ step) for lane in range(lanes)]
         for m in list(held):
             held[m ^ step] = tuple(lax.ppermute(part, "expert", order) for part in held[m])
         step //= 2
     return held
+
+
+def halve(blocks, axis, step):
+    size = lax.axis_size(axis)
+    bit = (lax.axis_index(axis) // step) % 2
+    pairs = blocks.reshape((blocks.shape[0] // 2, 2) + blocks.shape[1:])
+    given = lax.dynamic_index_in_dim(pairs, 1 - bit, axis=1, keepdims=False)
+    kept = lax.dynamic_index_in_dim(pairs, bit, axis=1, keepdims=False)
+    order = [(place, place ^ step) for place in range(size)]
+    return kept + lax.ppermute(given.astype(jnp.bfloat16), axis, order).astype(jnp.float32)
+
+
+def sum_lanes(blocks):
+    step = 1
+    while step < lax.axis_size("expert"):
+        blocks = halve(blocks, "expert", step)
+        step *= 2
+    return blocks[0]
+
+
+def sum_line(blocks):
+    size = lax.axis_size("seq")
+    count = blocks.shape[0]
+    inner = size // count
+    place = lax.axis_index("seq") // inner
+    result = lax.dynamic_index_in_dim(blocks, place, axis=0, keepdims=False)
+    for way in (1, -1):
+        moving = None
+        for far in range(count - 1, 0, -1):
+            block = lax.dynamic_index_in_dim(
+                blocks, jnp.clip(place + way * far, 0, count - 1), axis=0, keepdims=False
+            )
+            moving = block if moving is None else block + moving
+            order = [
+                (index, index + way * inner)
+                for index in range(size)
+                if 0 <= index // inner + way * far < count
+            ]
+            moving = lax.ppermute(moving.astype(jnp.bfloat16), "seq", order).astype(jnp.float32)
+        result = result + moving
+    return result
+
+
+def sum_shards(total):
+    size = lax.axis_size("seq")
+    part = total.shape[0] // size
+    half = total.shape[1] // 2
+    first = halve(total[:, :half].reshape(size, part, half), "seq", 1)
+    first = sum_line(first)
+    second = sum_line(total[:, half:].reshape(size // 2, 2 * part, half))
+    second = halve(second.reshape(2, part, half), "seq", 1)[0]
+    return jnp.concatenate([first, second], axis=1)
 
 
 def lane_gates(routes, route_gates):
@@ -177,10 +237,8 @@
             gate = lax.dynamic_index_in_dim(gates, lane ^ m, axis=1, keepdims=False)
             gate = gate[:, index * part : (index + 1) * part].reshape(-1, 1)
             total += gate * expert_rows(tokens, up[0], down[0]).astype(jnp.float32)
-        results.append(
-            lax.psum_scatter(total.astype(jnp.bfloat16), "seq", scatter_dimension=0, tiled=True)
-        )
-    return jnp.concatenate(results, axis=0).astype(jnp.float32)
+        results.append(sum_shards(total))
+    return jnp.concatenate(results, axis=0)
 
 
 def routed_by_pairs(expert_in, routes, route_gates, expert_up, expert_down):
@@ -238,25 +296,35 @@
     by_gather = experts <= 4 * routes.shape[1]
     if by_gather:
         gates = lane_gates(routes, route_gates)
-        weights = lane_weights((expert_up, expert_down))
+        middle = expert_up.shape[1] // 2
+        far_up = [far_lane(expert_up[:, :middle]), far_lane(expert_up[:, middle:])]
+        far_down = far_lane(expert_down)
     transit, offset, exposure, direct = block_terms(
         query_rows, key_rows, value_rows, log_decay, write_rate
     )
     pair, weights_in, local_outs = shard_chain(transit, offset, exposure, direct)
     heads = pair.shape[0]
     value_width = local_outs.shape[-1]
+    if by_gather:
+        pair, far_up[0] = tie(pair, far_up[0])
     incoming = incoming_states(pair)
+    if by_gather:
+        incoming, far_up[1] = tie(incoming, far_up[1])
     head_out = local_outs + jnp.einsum("hnsd,hde->hnse", weights_in, incoming, precision=precise)
     head_norm = head_out * lax.rsqrt(jnp.mean(head_out * head_out, axis=-1, keepdims=True) + 1e-06)
     head_norm = head_norm.astype(jnp.bfloat16)
     tokens = query_rows.shape[0]
     head_norm = jnp.transpose(head_norm, (1, 2, 0, 3)).reshape(tokens, heads * value_width)
-    attended = lax.psum_scatter(
-        jnp.dot(head_norm, output_weight, preferred_element_type=jnp.float32).astype(jnp.bfloat16),
-        "expert",
-        scatter_dimension=0,
-        tiled=True,
-    ).astype(jnp.float32)
+    projected = jnp.dot(head_norm, output_weight, preferred_element_type=jnp.float32)
+    attended = sum_lanes(projected.reshape((-1,) + residual.shape))
+    if by_gather:
+        attended, far_down = tie(attended, far_down)
+        weights = lane_weights(
+            {
+                0: (expert_up, expert_down),
+                lax.axis_size("expert") // 2: (jnp.concatenate(far_up, axis=1), far_down),
+            }
+        )
     mixed = (residual.astype(jnp.float32) + attended).astype(jnp.bfloat16)
     mixed_wide = mixed.astype(jnp.float32)
     expert_in = (

time: 509 us -> 469 us (0.921)
  waiting for transfers between devices: 295 us -> 152 us
  starting transfers between devices: 18.2 us -> 102 us
  local copies, waits for them, and re-layouts: 23.7 us -> 36.6 us
    reduce_scatter x3 -> x0, waiting for transfers between devices: 155 us -> none  [the longest x2 111 us: routed_by_gather(): lax.psum_scatter(total.astype(jnp.bfloat16), 'seq', scatter_dimension=0,...]
    ppermute x6 -> x4, waiting for transfers between devices: 105 us -> 0.01 us  [lane_weights(): lax.ppermute(part, 'expert', order)]
    ppermute x0 -> x33, starting transfers between devices: none -> 86.7 us  [the longest x24 77 us: sum_line(): lax.ppermute(moving.astype(jnp.bfloat16), 'seq', order).astype(jnp.float32)]
    ppermute x0 -> x33, waiting for transfers between devices: none -> 81.6 us  [the longest x6 61.9 us: halve(): lax.ppermute(given.astype(jnp.bfloat16), axis, order).astype(jnp.float32)]
    all_gather x2, waiting for transfers between devices: 20.1 us -> 49 us  [routed_by_gather(): tokens = lax.all_gather(own, 'seq', axis=0, tiled=True)]
    slice x0 -> x3, local copies, waits for them, and re-layouts: none -> 5.82 us  [the longest x1 5.21 us: per_device(): far_up = [far_lane(expert_up[:, :middle]), far_lane(expert_up[:, middle:])]]
    all_to_all x1, waiting for transfers between devices: 6.38 us -> 12.1 us  [incoming_states(): mine = lax.all_to_all(pair, 'seq', split_axis=0, concat_axis=0, tiled=True)]
    unnamed x82 -> x65, local copies, waits for them, and re-layouts: 19.9 us -> 21.8 us
  transfers between devices with their start and end apart: 14 -> 42, of which waited for: 9 -> 15; matrix products, arithmetic and copies ran while one was open for 19% -> 35% of each run, Pallas kernels for 0% -> 0%
where the time goes in v3:
time: 469 us; the launch traced here: 463 us
  waiting for transfers between devices  152 us (32%)
  matrix products  141 us (30%)
  starting transfers between devices  102 us (22%)
  local copies, waits for them, and re-layouts  36.6 us (8%)
  other arithmetic  16.1 us (3%)
  between operations  15.2 us (3%)
    ppermute x24, starting transfers between devices, sum_line(): lax.ppermute(moving.astype(jnp.bfloat16), 'seq', order).astype(jnp.float32)  77 us
    ppermute x6, waiting for transfers between devices, halve(): lax.ppermute(given.astype(jnp.bfloat16), axis, order).astype(jnp.float32)  61.9 us
    all_gather x2, waiting for transfers between devices, routed_by_gather(): tokens = lax.all_gather(own, 'seq', axis=0, tiled=True)  49 us
    dot_general x8, matrix products, expert_rows(): gate_up = jnp.dot(rows_in, expert_up, preferred_element_type=jnp.float32)  37.7 us
    dot_general x8, matrix products, expert_rows(): jnp.dot(hidden, expert_down, preferred_element_type=jnp.float32)  27.1 us
    unnamed x65, local copies, waits for them, and re-layouts  21.8 us
    ppermute x24, waiting for transfers between devices, sum_line(): lax.ppermute(moving.astype(jnp.bfloat16), 'seq', order).astype(jnp.float32)  19.7 us
    all_to_all x1, waiting for transfers between devices, incoming_states(): mine = lax.all_to_all(pair, 'seq', split_axis=0, concat_axis=0, tiled=True)  12.1 us
  transfers between devices with their start and end apart: 42, of which 15 were waited for; matrix products, arithmetic and copies ran while one was open for 35% of the time, Pallas kernels for 0%

profile of v3, /device:TPU:0, one launch (start us, length us, event | category | flops | bytes accessed | tf_op | source)
XLA Modules:
  0.0 462.9 jit_solution(3489136543421442824)
XLA Ops:
  6.5 5.2 %fusion.222 = (bf16[1,1152,1024]{2,1,0:T(8,128)(2,1)}, bf16[1,1152,1024]{2,1,0:T(8,128)(2,1)}) fusion(bf16[1,2304,1024]{2,1,0:T(8,128)(2,1)} %param.36), kind=kLoop, calls=%fused_computation.393 | loop fusion | bytes 9437184 | tf_op jit(solution)/shard_map/slice | solution.py:300
  11.7 2.9 collective-permute-start
  19.6 5.7 %multiply_select_fusion = f32[8,8,64,64]{3,2,1,0:T(8,128)S(1)} fusion(f32[8,8,64,128]{3,1,2,0:T(8,128)S(1)} %fusion.36, f32[8,64,8,128]{3,2,1,0:T(8,128)} %bitcast.485, f32[8,8,64]{2,1,0:T(8,128)S(1)} %bitcast.514, f32[8,8,64]{2,1,0:T(8,128)S(1)} %add_rsqrt_fusion.1, f32[8,8,128]{2,1,0:T(8,128)S(1)} %get-tuple-element.131, ...), kind=kOutput, calls=%fused_computation.81 | convolution fusion | flops 204996608 | bytes 5312512 | tf_op jit(solution)/shard_map/hnsd,hntd->hnst/dot_general | solution.py:53
  42.1 2.4 fusion.20
  44.6 4.3 fusion.61
  48.9 5.7 %multiply_subtract_fusion = f32[8,8,128,128]{3,2,1,0:T(8,128)S(1)} fusion(f32[8,8,128]{2,1,0:T(8,128)S(1)} %get-tuple-element.130, f32[128,128]{1,0:T(8,128)S(1)} %fusion.195, f32[8,8,64,256]{3,2,1,0:T(8,128)S(1)} %fusion.20, f32[8,8,64,128]{3,1,2,0:T(8,128)S(1)} %fusion.36, f32[8,64,8,128]{3,2,1,0:T(8,128)S(1)} %bitcast.488, ...), kind=kOutput, calls=%fused_computation.34 | convolution fusion | flops 406323200 | bytes 10649600 | tf_op jit(solution)/shard_map/hncd,hnce->hnde/dot_general | solution.py:73
  64.6 3.2 copy-done.11
  67.8 6.6 %all-to-all-start = ((f32[8,128,256]{2,1,0:T(8,128)}), f32[8,128,256]{2,1,0:T(8,128)}, u32[]{:S(2)}, u32[]{:S(2)}) async-start(f32[8,128,256]{2,1,0:T(8,128)} %copy-done.14), calls=%async_computation | async-start | bytes 2097152 | tf_op jit(solution)/shard_map/all_to_all | solution.py:107
  75.6 2.8 bitcast_dynamic-update-slice_fusion.1
  78.4 4.2 fusion.56
  82.6 2.6 fusion.64
  85.2 2.6 fusion.59
  87.8 12.1 %all-to-all-done = f32[8,128,256]{2,1,0:T(8,128)} async-done(((f32[8,128,256]{2,1,0:T(8,128)}), f32[8,128,256]{2,1,0:T(8,128)}, u32[]{:S(2)}, u32[]{:S(2)}) %all-to-all-start) | async-done | bytes 1048608 | tf_op jit(solution)/shard_map/all_to_all | solution.py:107
  101.5 1.7 bitcast_dynamic-update-slice_fusion.11
  103.2 1.7 bitcast_dynamic-update-slice_fusion.10
  108.3 1.7 bitcast_dynamic-update-slice_fusion.7
  111.6 4.1 all-to-all-start.1
  117.8 9.4 %fusion = f32[8,8,64,256]{3,2,1,0:T(8,128)} fusion(f32[8,8,128,256]{3,2,0,1:T(8,128)} %bitcast_dynamic-update-slice_fusion, f32[8,8,64,128]{3,2,1,0:T(8,128)} %fusion.64, f32[8,64,8,128]{3,2,1,0:T(8,128)S(1)} %bitcast.492, f32[8,8,64,128]{3,1,2,0:T(8,128)S(1)} %fusion.36, f32[8,8,64]{2,1,0:T(8,128)S(1)} %add_rsqrt_fusion.2), kind=kOutput, calls=%fused_computation | convolution fusion | flops 806879232 | bytes 18890752 | tf_op jit(solution)/shard_map/hnsd,hnde->hnse/dot_general | solution.py:98
  127.2 2.6 all-to-all-done.1
  129.8 4.7 %multiply_reduce_fusion = (f32[8,8,64]{2,1,0:T(8,128)S(1)}, f32[8,8,64,128]{3,2,1,0:T(8,128)S(1)}) fusion(f32[8,128,128]{2,1,0:T(8,128)} %all-to-all-done.1, f32[8,8,64,256]{3,2,1,0:T(8,128)} %fusion, f32[8,8,64,128]{3,2,1,0:T(8,128)} %fusion.59), kind=kOutput, calls=%fused_computation.63 | convolution fusion | flops 404746240 | bytes 8929280 | tf_op jit(solution)/shard_map/hnsd,hde->hnse/dot_general | solution.py:313
  136.7 4.9 %fusion.2 = f32[2,2,128,2304]{3,2,1,0:T(8,128)S(1)} fusion(bf16[2,2,128,1024]{3,2,1,0:T(8,128)(2,1)S(1)} %dot_general.189, bf16[1024,2304]{1,0:T(8,128)(2,1)} %param.33), kind=kOutput, calls=%fused_computation.2 | convolution fusion | flops 2415919104 | bytes 10485760 | tf_op jit(solution)/shard_map/dot_general | solution.py:318
  141.6 2.2 copy-done.15
  146.8 1.9 bitcast_add_fusion
  150.3 60.3 %collective-permute-done.3 = bf16[1,128,2304]{2,1,0:T(8,128)(2,1)} collective-permute-done((bf16[1,128,2304]{2,1,0:T(8,128)(2,1)S(1)}, bf16[1,128,2304]{2,1,0:T(8,128)(2,1)}, u32[]{:S(2)}, u32[]{:S(2)}) %collective-permute-start.3) | collective-permute-done | bytes 589856 | tf_op jit(solution)/shard_map/ppermute | solution.py:172
  213.2 3.2 constant_dynamic-update-slice_fusion.2
  216.5 3.3 constant_dynamic-update-slice_fusion.1
  220.9 3.6 all-to-all-start.2
  224.8 6.6 %all-to-all-done.2 = f32[8,4,128]{2,1,0:T(4,128)S(1)} async-done(((f32[8,4,128]{2,1,0:T(4,128)}), f32[8,4,128]{2,1,0:T(4,128)S(1)}, u32[]{:S(2)}, u32[]{:S(2)}) %all-to-all-start.2) | async-done | bytes 16416 | tf_op jit(solution)/shard_map/all_to_all | solution.py:223
  232.3 32.4 %all-gather.3.cloned.1.call-done = bf16[512,2304]{1,0:T(8,128)(2,1)} async-done(((bf16[64,2304]{1,0:T(8,128)(2,1)}), bf16[512,2304]{1,0:T(8,128)(2,1)}) %all-gather.3.cloned.1.call-update) | async-done | bytes 2359312 | tf_op jit(solution)/shard_map/all_gather | solution.py:234
  264.7 5.6 %fusion.14 = f32[512,1024]{1,0:T(8,128)S(1)} fusion(bf16[512,2304]{1,0:T(8,128)(2,1)} %all-gather.3.cloned.1.call-done, bf16[1,2304,1024]{2,1,0:T(8,128)(2,1)} %constant_dynamic-update-slice_fusion.1), kind=kOutput, calls=%fused_computation.14 | convolution fusion | flops 2415919104 | bytes 9175040 | tf_op jit(solution)/shard_map/dot_general | solution.py:138
  270.3 3.4 convolution_convert_fusion.6
  273.7 4.5 fusion.18
  278.2 3.2 convolution_convert_fusion.7
  281.4 4.5 fusion.10
  285.9 3.2 convolution_convert_fusion.5
  289.2 4.5 fusion.6
  293.6 3.7 multiply_add_fusion.1
  300.9 4.1 collective-permute-start.16
  306.4 16.6 %all-gather.5.cloned.1.call-done = bf16[512,2304]{1,0:T(8,128)(2,1)} async-done(((bf16[64,2304]{1,0:T(8,128)(2,1)}), bf16[512,2304]{1,0:T(8,128)(2,1)}) %all-gather.5.cloned.1.call-update) | async-done | bytes 2359312 | tf_op jit(solution)/shard_map/all_gather | solution.py:234
  323.0 5.3 %fusion.12 = f32[512,1024]{1,0:T(8,128)S(1)} fusion(bf16[512,2304]{1,0:T(8,128)(2,1)} %all-gather.5.cloned.1.call-done, bf16[1,2304,1024]{2,1,0:T(8,128)(2,1)} %constant_dynamic-update-slice_fusion.1), kind=kOutput, calls=%fused_computation.12 | convolution fusion | flops 2415919104 | bytes 9175040 | tf_op jit(solution)/shard_map/dot_general | solution.py:138
  328.3 3.4 convolution_convert_fusion.2
  331.7 4.5 fusion.16
  336.2 3.2 convolution_convert_fusion.3
  339.4 4.5 fusion.4
  343.9 4.5 fusion.8
  348.3 3.2 convolution_convert_fusion.1
  351.6 3.7 multiply_add_fusion
  356.4 4.8 %collective-permute-start.30 = (bf16[128,1152]{1,0:T(8,128)(2,1)S(1)}, bf16[128,1152]{1,0:T(8,128)(2,1)S(1)}, u32[]{:S(2)}, u32[]{:S(2)}) collective-permute-start(bf16[128,1152]{1,0:T(8,128)(2,1)S(1)} %get-tuple-element.127), channel_id=1, source_target_pairs={{0,8},{4,12},{1,9},{5,13},{2,10},{6,14},{3,11},{7,15}} | collective-permute-start | bytes 884744 | tf_op jit(solution)/shard_map/ppermute | solution.py:201
  362.9 2.9 collective-permute-done.30
  365.8 4.4 collective-permute-start.17
  370.3 2.1 collective-permute-start.31
  372.4 4.7 %collective-permute-done.17 = bf16[128,1152]{1,0:T(8,128)(2,1)S(1)} collective-permute-done((bf16[128,1152]{1,0:T(8,128)(2,1)S(1)}, bf16[128,1152]{1,0:T(8,128)(2,1)S(1)}, u32[]{:S(2)}, u32[]{:S(2)}) %collective-permute-start.17) | collective-permute-done | bytes 294944 | tf_op jit(solution)/shard_map/ppermute | solution.py:201
  378.9 5.0 %collective-permute-start.18 = (bf16[128,1152]{1,0:T(8,128)(2,1)S(1)}, bf16[128,1152]{1,0:T(8,128)(2,1)S(1)}, u32[]{:S(2)}, u32[]{:S(2)}) collective-permute-start(bf16[128,1152]{1,0:T(8,128)(2,1)S(1)} %get-tuple-element.121), channel_id=1, source_target_pairs={{0,8},{4,12},{8,16},{12,20},{16,24},{20,28},{1,9},{5,13},{9,17},{1... | collective-permute-start | bytes 884744 | tf_op jit(solution)/shard_map/ppermute | solution.py:201
  384.7 5.2 %collective-permute-start.32 = (bf16[128,1152]{1,0:T(8,128)(2,1)S(1)}, bf16[128,1152]{1,0:T(8,128)(2,1)S(1)}, u32[]{:S(2)}, u32[]{:S(2)}) collective-permute-start(bf16[128,1152]{1,0:T(8,128)(2,1)S(1)} %get-tuple-element.125), channel_id=1, source_target_pairs={{0,8},{4,12},{8,16},{12,20},{16,24},{20,28},{1,9},{5,13},{9,17},{1... | collective-permute-start | bytes 884744 | tf_op jit(solution)/shard_map/ppermute | solution.py:201
  391.2 4.5 collective-permute-start.10
  395.9 3.2 collective-permute-done.10
  399.1 4.4 collective-permute-start.24
  403.5 4.2 collective-permute-done.24
  409.2 4.4 collective-permute-start.11
  413.6 1.9 collective-permute-start.25
  420.4 23.0 %collective-permute-start.12 = (bf16[64,1152]{1,0:T(8,128)(2,1)S(1)}, bf16[64,1152]{1,0:T(8,128)(2,1)S(1)}, u32[]{:S(2)}, u32[]{:S(2)}) collective-permute-start(bf16[64,1152]{1,0:T(8,128)(2,1)S(1)} %get-tuple-element.132), channel_id=1, source_target_pairs={{0,8},{4,12},{8,16},{12,20},{16,24},{20,28},{1,9},{5,13},{9,17},{1... | collective-permute-start | bytes 442376 | tf_op jit(solution)/shard_map/ppermute | solution.py:201
  443.5 1.9 collective-permute-start.26
  450.4 2.0 collective-permute-done.15
  452.5 2.0 collective-permute-done.29
  (226 shorter events, 76.8 us)
Async XLA Ops:
  6.5 8.3 %copy-start.16 = (f32[512,1024]{1,0:T(8,128)S(1)}, f32[512,1024]{1,0:T(8,128)}, u32[]{:S(2)}) copy-start(f32[512,1024]{1,0:T(8,128)} %param.31) | copy-start | bytes 6291460
  11.7 56.1 %collective-permute-start = (bf16[1,1152,1024]{2,1,0:T(8,128)(2,1)}, bf16[1,1152,1024]{2,1,0:T(8,128)(2,1)}, u32[]{:S(2)}, u32[]{:S(2)}) collective-permute-start(bf16[1,1152,1024]{2,1,0:T(8,128)(2,1)} %get-tuple-element.120), channel_id=1, source_target_pairs={{0,2},{1,3},{2,0},{3,1},{4,6},{5,7},{6,4},{7,5},{8,10},{9,11},{10,... | collective-permute-start | bytes 7077896 | tf_op jit(solution)/shard_map/ppermute | solution.py:151
  14.7 112.5 %collective-permute-start.1 = (bf16[1,1152,1024]{2,1,0:T(8,128)(2,1)}, bf16[1,1152,1024]{2,1,0:T(8,128)(2,1)}, u32[]{:S(2)}, u32[]{:S(2)}) collective-permute-start(bf16[1,1152,1024]{2,1,0:T(8,128)(2,1)} %get-tuple-element.119), channel_id=1, source_target_pairs={{0,2},{1,3},{2,0},{3,1},{4,6},{5,7},{6,4},{7,5},{8,10},{9,11},{10,... | collective-permute-start | bytes 7077896 | tf_op jit(solution)/shard_map/ppermute | solution.py:151
  15.3 1.4 copy-start.17
  17.4 2.0 copy-start.21
  37.4 1.5 copy-start.18
  39.1 1.6 copy-start.1
  44.5 4.3 copy-start.3
  59.6 2.1 copy-start.8
  60.3 2.1 copy-start.5
  64.6 3.2 copy-start.11
  67.8 32.0 %all-to-all-start = ((f32[8,128,256]{2,1,0:T(8,128)}), f32[8,128,256]{2,1,0:T(8,128)}, u32[]{:S(2)}, u32[]{:S(2)}) async-start(f32[8,128,256]{2,1,0:T(8,128)} %copy-done.14), calls=%async_computation | async-start | bytes 2097152 | tf_op jit(solution)/shard_map/all_to_all | solution.py:107
  74.5 3.9 copy-start.2
  74.5 3.9 copy-start.6
  78.4 4.2 copy-start.4
  87.8 28.0 %copy-start.10 = (f32[8,128,256]{2,1,0:T(8,128)S(1)}, f32[8,128,256]{2,1,0:T(8,128)}, u32[]{:S(2)}) copy-start(f32[8,128,256]{2,1,0:T(8,128)} %copy-done.9) | copy-start | bytes 3145732
  111.6 18.2 %all-to-all-start.1 = ((f32[8,128,128]{2,1,0:T(8,128)}), f32[8,128,128]{2,1,0:T(8,128)}, u32[]{:S(2)}, u32[]{:S(2)}) async-start(f32[8,128,128]{2,1,0:T(8,128)} %fusion.85), calls=%async_computation.1 | async-start | bytes 1048576 | tf_op jit(solution)/shard_map/all_to_all | solution.py:117
  115.8 148.9 %all-gather.3.cloned.1.call-start = ((), (), s32[]{:S(2)}) async-start(), calls=%async_computation.3 | async-start | bytes 2654208 | tf_op jit(solution)/shard_map/all_gather | solution.py:234
  115.8 2.0 copy-start.7
  141.6 2.2 copy-start.15
  143.9 2.9 collective-permute-start.2
  144.0 67.8 %collective-permute-start.4 = (bf16[1,512,2304]{2,1,0:T(8,128)(2,1)}, bf16[1,512,2304]{2,1,0:T(8,128)(2,1)}, u32[]{:S(2)}, u32[]{:S(2)}) collective-permute-start(bf16[1,512,2304]{2,1,0:T(8,128)(2,1)} %param.37), channel_id=1, source_target_pairs={{0,2},{1,3},{2,0},{3,1},{4,6},{5,7},{6,4},{7,5},{8,10},{9,11},{10,... | collective-permute-start | bytes 7077896 | tf_op jit(solution)/shard_map/ppermute | solution.py:151
  148.7 63.1 %copy-start.20 = (bf16[128,2304]{1,0:T(8,128)(2,1)S(1)}, bf16[128,2304]{1,0:T(8,128)(2,1)}, u32[]{:S(2)}) copy-start(bf16[128,2304]{1,0:T(8,128)(2,1)} %param.27) | copy-start | bytes 1769476
  148.8 61.8 %collective-permute-start.3 = (bf16[1,128,2304]{2,1,0:T(8,128)(2,1)S(1)}, bf16[1,128,2304]{2,1,0:T(8,128)(2,1)}, u32[]{:S(2)}, u32[]{:S(2)}) collective-permute-start(bf16[1,128,2304]{2,1,0:T(8,128)(2,1)S(1)} %dynamic-slice_convert_fusion.1), channel_id=1, source_target_pairs={{0,2},{1,3},{2,0},{3,1},{4,6},{5,7},{6,4},{7,5},{8,10},{9,11},{10,... | collective-permute-start | bytes 1769480 | tf_op jit(solution)/shard_map/ppermute | solution.py:172
  213.2 68.3 %collective-permute-start.5 = (bf16[1,2304,1024]{2,1,0:T(8,128)(2,1)}, bf16[1,2304,1024]{2,1,0:T(8,128)(2,1)}, u32[]{:S(2)}, u32[]{:S(2)}) collective-permute-start(bf16[1,2304,1024]{2,1,0:T(8,128)(2,1)} %param.36), channel_id=1, source_target_pairs={{0,1},{1,0},{2,3},{3,2},{4,5},{5,4},{6,7},{7,6},{8,9},{9,8},{10,11... | collective-permute-start | bytes 14155784 | tf_op jit(solution)/shard_map/ppermute | solution.py:160
  216.5 3.8 copy-start.22
  216.5 3.8 copy-start.23
  219.8 69.3 %collective-permute-start.7 = (bf16[1,2304,1024]{2,1,0:T(8,128)(2,1)}, bf16[1,2304,1024]{2,1,0:T(8,128)(2,1)}, u32[]{:S(2)}, u32[]{:S(2)}) collective-permute-start(bf16[1,2304,1024]{2,1,0:T(8,128)(2,1)} %constant_dynamic-update-slice_fusion.1), channel_id=1, source_target_pairs={{0,1},{1,0},{2,3},{3,2},{4,5},{5,4},{6,7},{7,6},{8,9},{9,8},{10,11... | collective-permute-start | bytes 14155784 | tf_op jit(solution)/shard_map/ppermute | solution.py:160
  220.9 10.4 %all-to-all-start.2 = ((f32[8,4,128]{2,1,0:T(4,128)}), f32[8,4,128]{2,1,0:T(4,128)S(1)}, u32[]{:S(2)}, u32[]{:S(2)}) async-start(f32[8,4,128]{2,1,0:T(4,128)} %bitcast.65), calls=%async_computation.2 | async-start | bytes 32768 | tf_op jit(solution)/shard_map/all_to_all | solution.py:223
  224.6 98.4 %all-gather.5.cloned.1.call-start = ((), (), s32[]{:S(2)}) async-start(), calls=%async_computation.4 | async-start | bytes 2654208 | tf_op jit(solution)/shard_map/all_gather | solution.py:234
  224.6 61.3 %collective-permute-start.6 = (bf16[1,512,2304]{2,1,0:T(8,128)(2,1)}, bf16[1,512,2304]{2,1,0:T(8,128)(2,1)}, u32[]{:S(2)}, u32[]{:S(2)}) collective-permute-start(bf16[1,512,2304]{2,1,0:T(8,128)(2,1)} %param.37), channel_id=1, source_target_pairs={{0,1},{1,0},{2,3},{3,2},{4,5},{5,4},{6,7},{7,6},{8,9},{9,8},{10,11... | collective-permute-start | bytes 7077896 | tf_op jit(solution)/shard_map/ppermute | solution.py:160
  232.3 61.4 %collective-permute-start.8 = (bf16[1,512,2304]{2,1,0:T(8,128)(2,1)}, bf16[1,512,2304]{2,1,0:T(8,128)(2,1)}, u32[]{:S(2)}, u32[]{:S(2)}) collective-permute-start(bf16[1,512,2304]{2,1,0:T(8,128)(2,1)} %collective-permute-done.4), channel_id=1, source_target_pairs={{0,1},{1,0},{2,3},{3,2},{4,5},{5,4},{6,7},{7,6},{8,9},{9,8},{10,11... | collective-permute-start | bytes 7077896 | tf_op jit(solution)/shard_map/ppermute | solution.py:160
  270.3 3.4 copy-start.24
  297.7 1.4 copy-start.12
  299.2 85.5 %collective-permute-start.9 = (bf16[4,64,1152]{2,1,0:T(8,128)(2,1)S(1)}, bf16[4,64,1152]{2,1,0:T(8,128)(2,1)}, u32[]{:S(2)}, u32[]{:S(2)}) collective-permute-start(bf16[4,64,1152]{2,1,0:T(8,128)(2,1)S(1)} %fusion.121), channel_id=1, source_target_pairs={{0,4},{4,0},{8,12},{12,8},{16,20},{20,16},{24,28},{28,24},{1,5},{5... | collective-permute-start | bytes 1769480 | tf_op jit(solution)/shard_map/ppermute | solution.py:172
  300.9 60.3 %collective-permute-start.16 = (bf16[128,1152]{1,0:T(8,128)(2,1)}, bf16[128,1152]{1,0:T(8,128)(2,1)}, u32[]{:S(2)}, u32[]{:S(2)}) collective-permute-start(bf16[128,1152]{1,0:T(8,128)(2,1)} %get-tuple-element.123), channel_id=1, source_target_pairs={{0,8},{4,12},{1,9},{5,13},{2,10},{6,14},{3,11},{7,15}} | collective-permute-start | bytes 884744 | tf_op jit(solution)/shard_map/ppermute | solution.py:201
  305.0 65.3 %collective-permute-start.19 = (bf16[128,1152]{1,0:T(8,128)(2,1)}, bf16[128,1152]{1,0:T(8,128)(2,1)}, u32[]{:S(2)}, u32[]{:S(2)}) collective-permute-start(bf16[128,1152]{1,0:T(8,128)(2,1)} %get-tuple-element.124), channel_id=1, source_target_pairs={{24,16},{28,20},{25,17},{29,21},{26,18},{30,22},{27,19},{31,23}} | collective-permute-start | bytes 884744 | tf_op jit(solution)/shard_map/ppermute | solution.py:201
  328.3 3.4 copy-start.25
  355.7 35.5 %collective-permute-start.23 = (bf16[4,64,1152]{2,1,0:T(8,128)(2,1)S(1)}, bf16[4,64,1152]{2,1,0:T(8,128)(2,1)S(1)}, u32[]{:S(2)}, u32[]{:S(2)}) collective-permute-start(bf16[4,64,1152]{2,1,0:T(8,128)(2,1)S(1)} %fusion.122), channel_id=1, source_target_pairs={{0,4},{4,0},{8,12},{12,8},{16,20},{20,16},{24,28},{28,24},{1,5},{5... | collective-permute-start | bytes 1769480 | tf_op jit(solution)/shard_map/ppermute | solution.py:172
  356.4 9.5 %collective-permute-start.30 = (bf16[128,1152]{1,0:T(8,128)(2,1)S(1)}, bf16[128,1152]{1,0:T(8,128)(2,1)S(1)}, u32[]{:S(2)}, u32[]{:S(2)}) collective-permute-start(bf16[128,1152]{1,0:T(8,128)(2,1)S(1)} %get-tuple-element.127), channel_id=1, source_target_pairs={{0,8},{4,12},{1,9},{5,13},{2,10},{6,14},{3,11},{7,15}} | collective-permute-start | bytes 884744 | tf_op jit(solution)/shard_map/ppermute | solution.py:201
  361.2 17.7 %collective-permute-start.33 = (bf16[128,1152]{1,0:T(8,128)(2,1)S(1)}, bf16[128,1152]{1,0:T(8,128)(2,1)S(1)}, u32[]{:S(2)}, u32[]{:S(2)}) collective-permute-start(bf16[128,1152]{1,0:T(8,128)(2,1)S(1)} %get-tuple-element.128), channel_id=1, source_target_pairs={{24,16},{28,20},{25,17},{29,21},{26,18},{30,22},{27,19},{31,23}} | collective-permute-start | bytes 884744 | tf_op jit(solution)/shard_map/ppermute | solution.py:201
  365.8 11.3 %collective-permute-start.17 = (bf16[128,1152]{1,0:T(8,128)(2,1)S(1)}, bf16[128,1152]{1,0:T(8,128)(2,1)S(1)}, u32[]{:S(2)}, u32[]{:S(2)}) collective-permute-start(bf16[128,1152]{1,0:T(8,128)(2,1)S(1)} %fusion.130), channel_id=1, source_target_pairs={{0,8},{4,12},{8,16},{12,20},{1,9},{5,13},{9,17},{13,21},{2,10},{6,... | collective-permute-start | bytes 884744 | tf_op jit(solution)/shard_map/ppermute | solution.py:201
  370.3 19.6 %copy-start.13 = (f32[512,1152]{1,0:T(8,128)S(1)}, f32[512,1152]{1,0:T(8,128)}, u32[]{:S(2)}) copy-start(f32[512,1152]{1,0:T(8,128)} %copy-done.12) | copy-start | bytes 7077892
  370.3 13.6 %collective-permute-start.31 = (bf16[128,1152]{1,0:T(8,128)(2,1)S(1)}, bf16[128,1152]{1,0:T(8,128)(2,1)S(1)}, u32[]{:S(2)}, u32[]{:S(2)}) collective-permute-start(bf16[128,1152]{1,0:T(8,128)(2,1)S(1)} %fusion.125), channel_id=1, source_target_pairs={{0,8},{4,12},{8,16},{12,20},{1,9},{5,13},{9,17},{13,21},{2,10},{6,... | collective-permute-start | bytes 884744 | tf_op jit(solution)/shard_map/ppermute | solution.py:201
  378.2 30.2 %collective-permute-start.20 = (bf16[128,1152]{1,0:T(8,128)(2,1)S(1)}, bf16[128,1152]{1,0:T(8,128)(2,1)S(1)}, u32[]{:S(2)}, u32[]{:S(2)}) collective-permute-start(bf16[128,1152]{1,0:T(8,128)(2,1)S(1)} %get-tuple-element.122), channel_id=1, source_target_pairs={{16,8},{20,12},{24,16},{28,20},{17,9},{21,13},{25,17},{29,21},{18,... | collective-permute-start | bytes 884744 | tf_op jit(solution)/shard_map/ppermute | solution.py:201
  378.9 64.6 %collective-permute-start.18 = (bf16[128,1152]{1,0:T(8,128)(2,1)S(1)}, bf16[128,1152]{1,0:T(8,128)(2,1)S(1)}, u32[]{:S(2)}, u32[]{:S(2)}) collective-permute-start(bf16[128,1152]{1,0:T(8,128)(2,1)S(1)} %get-tuple-element.121), channel_id=1, source_target_pairs={{0,8},{4,12},{8,16},{12,20},{16,24},{20,28},{1,9},{5,13},{9,17},{1... | collective-permute-start | bytes 884744 | tf_op jit(solution)/shard_map/ppermute | solution.py:201
  384.0 25.1 %collective-permute-start.34 = (bf16[128,1152]{1,0:T(8,128)(2,1)S(1)}, bf16[128,1152]{1,0:T(8,128)(2,1)S(1)}, u32[]{:S(2)}, u32[]{:S(2)}) collective-permute-start(bf16[128,1152]{1,0:T(8,128)(2,1)S(1)} %get-tuple-element.126), channel_id=1, source_target_pairs={{16,8},{20,12},{24,16},{28,20},{17,9},{21,13},{25,17},{29,21},{18,... | collective-permute-start | bytes 884744 | tf_op jit(solution)/shard_map/ppermute | solution.py:201
  384.7 62.1 %collective-permute-start.32 = (bf16[128,1152]{1,0:T(8,128)(2,1)S(1)}, bf16[128,1152]{1,0:T(8,128)(2,1)S(1)}, u32[]{:S(2)}, u32[]{:S(2)}) collective-permute-start(bf16[128,1152]{1,0:T(8,128)(2,1)S(1)} %get-tuple-element.125), channel_id=1, source_target_pairs={{0,8},{4,12},{8,16},{12,20},{16,24},{20,28},{1,9},{5,13},{9,17},{1... | collective-permute-start | bytes 884744 | tf_op jit(solution)/shard_map/ppermute | solution.py:201
  391.2 7.9 %collective-permute-start.10 = (bf16[64,1152]{1,0:T(8,128)(2,1)S(1)}, bf16[64,1152]{1,0:T(8,128)(2,1)S(1)}, u32[]{:S(2)}, u32[]{:S(2)}) collective-permute-start(bf16[64,1152]{1,0:T(8,128)(2,1)S(1)} %get-tuple-element.134), channel_id=1, source_target_pairs={{0,8},{4,12},{1,9},{5,13},{2,10},{6,14},{3,11},{7,15}} | collective-permute-start | bytes 442376 | tf_op jit(solution)/shard_map/ppermute | solution.py:201
  399.1 8.6 %collective-permute-start.24 = (bf16[64,1152]{1,0:T(8,128)(2,1)S(1)}, bf16[64,1152]{1,0:T(8,128)(2,1)S(1)}, u32[]{:S(2)}, u32[]{:S(2)}) collective-permute-start(bf16[64,1152]{1,0:T(8,128)(2,1)S(1)} %get-tuple-element.138), channel_id=1, source_target_pairs={{0,8},{4,12},{1,9},{5,13},{2,10},{6,14},{3,11},{7,15}} | collective-permute-start | bytes 442376 | tf_op jit(solution)/shard_map/ppermute | solution.py:201
  407.7 5.9 %collective-permute-start.13 = (bf16[64,1152]{1,0:T(8,128)(2,1)S(1)}, bf16[64,1152]{1,0:T(8,128)(2,1)S(1)}, u32[]{:S(2)}, u32[]{:S(2)}) collective-permute-start(bf16[64,1152]{1,0:T(8,128)(2,1)S(1)} %get-tuple-element.135), channel_id=1, source_target_pairs={{24,16},{28,20},{25,17},{29,21},{26,18},{30,22},{27,19},{31,23}} | collective-permute-start | bytes 442376 | tf_op jit(solution)/shard_map/ppermute | solution.py:201
  408.4 9.2 %collective-permute-start.27 = (bf16[64,1152]{1,0:T(8,128)(2,1)S(1)}, bf16[64,1152]{1,0:T(8,128)(2,1)S(1)}, u32[]{:S(2)}, u32[]{:S(2)}) collective-permute-start(bf16[64,1152]{1,0:T(8,128)(2,1)S(1)} %get-tuple-element.139), channel_id=1, source_target_pairs={{24,16},{28,20},{25,17},{29,21},{26,18},{30,22},{27,19},{31,23}} | collective-permute-start | bytes 442376 | tf_op jit(solution)/shard_map/ppermute | solution.py:201
  409.2 7.1 %collective-permute-start.11 = (bf16[64,1152]{1,0:T(8,128)(2,1)S(1)}, bf16[64,1152]{1,0:T(8,128)(2,1)S(1)}, u32[]{:S(2)}, u32[]{:S(2)}) collective-permute-start(bf16[64,1152]{1,0:T(8,128)(2,1)S(1)} %fusion.186), channel_id=1, source_target_pairs={{0,8},{4,12},{8,16},{12,20},{1,9},{5,13},{9,17},{13,21},{2,10},{6,... | collective-permute-start | bytes 442376 | tf_op jit(solution)/shard_map/ppermute | solution.py:201
  413.6 5.2 %collective-permute-start.25 = (bf16[64,1152]{1,0:T(8,128)(2,1)S(1)}, bf16[64,1152]{1,0:T(8,128)(2,1)S(1)}, u32[]{:S(2)}, u32[]{:S(2)}) collective-permute-start(bf16[64,1152]{1,0:T(8,128)(2,1)S(1)} %fusion.180), channel_id=1, source_target_pairs={{0,8},{4,12},{8,16},{12,20},{1,9},{5,13},{9,17},{13,21},{2,10},{6,... | collective-permute-start | bytes 442376 | tf_op jit(solution)/shard_map/ppermute | solution.py:201
  416.2 29.2 %collective-permute-start.21 = (bf16[128,1152]{1,0:T(8,128)(2,1)S(1)}, bf16[128,1152]{1,0:T(8,128)(2,1)S(1)}, u32[]{:S(2)}, u32[]{:S(2)}) collective-permute-start(bf16[128,1152]{1,0:T(8,128)(2,1)S(1)} %fusion.129), channel_id=1, source_target_pairs={{8,0},{12,4},{16,8},{20,12},{24,16},{28,20},{9,1},{13,5},{17,9},{2... | collective-permute-start | bytes 884744 | tf_op jit(solution)/shard_map/ppermute | solution.py:201
  417.6 30.5 %collective-permute-start.35 = (bf16[128,1152]{1,0:T(8,128)(2,1)S(1)}, bf16[128,1152]{1,0:T(8,128)(2,1)S(1)}, u32[]{:S(2)}, u32[]{:S(2)}) collective-permute-start(bf16[128,1152]{1,0:T(8,128)(2,1)S(1)} %fusion.124), channel_id=1, source_target_pairs={{8,0},{12,4},{16,8},{20,12},{24,16},{28,20},{9,1},{13,5},{17,9},{2... | collective-permute-start | bytes 884744 | tf_op jit(solution)/shard_map/ppermute | solution.py:201
  418.9 0.7 collective-permute-start.14
  419.7 0.7 collective-permute-start.28
  420.4 29.2 %collective-permute-start.12 = (bf16[64,1152]{1,0:T(8,128)(2,1)S(1)}, bf16[64,1152]{1,0:T(8,128)(2,1)S(1)}, u32[]{:S(2)}, u32[]{:S(2)}) collective-permute-start(bf16[64,1152]{1,0:T(8,128)(2,1)S(1)} %get-tuple-element.132), channel_id=1, source_target_pairs={{0,8},{4,12},{8,16},{12,20},{16,24},{20,28},{1,9},{5,13},{9,17},{1... | collective-permute-start | bytes 442376 | tf_op jit(solution)/shard_map/ppermute | solution.py:201
  443.5 9.0 %collective-permute-start.26 = (bf16[64,1152]{1,0:T(8,128)(2,1)S(1)}, bf16[64,1152]{1,0:T(8,128)(2,1)S(1)}, u32[]{:S(2)}, u32[]{:S(2)}) collective-permute-start(bf16[64,1152]{1,0:T(8,128)(2,1)S(1)} %get-tuple-element.136), channel_id=1, source_target_pairs={{0,8},{4,12},{8,16},{12,20},{16,24},{20,28},{1,9},{5,13},{9,17},{1... | collective-permute-start | bytes 442376 | tf_op jit(solution)/shard_map/ppermute | solution.py:201
  445.4 7.0 %collective-permute-start.15 = (bf16[64,1152]{1,0:T(8,128)(2,1)S(1)}, bf16[64,1152]{1,0:T(8,128)(2,1)S(1)}, u32[]{:S(2)}, u32[]{:S(2)}) collective-permute-start(bf16[64,1152]{1,0:T(8,128)(2,1)S(1)} %fusion.185), channel_id=1, source_target_pairs={{8,0},{12,4},{16,8},{20,12},{24,16},{28,20},{9,1},{13,5},{17,9},{2... | collective-permute-start | bytes 442376 | tf_op jit(solution)/shard_map/ppermute | solution.py:201
  446.8 7.7 %collective-permute-start.29 = (bf16[64,1152]{1,0:T(8,128)(2,1)S(1)}, bf16[64,1152]{1,0:T(8,128)(2,1)S(1)}, u32[]{:S(2)}, u32[]{:S(2)}) collective-permute-start(bf16[64,1152]{1,0:T(8,128)(2,1)S(1)} %fusion.179), channel_id=1, source_target_pairs={{8,0},{12,4},{16,8},{20,12},{24,16},{28,20},{9,1},{13,5},{17,9},{2... | collective-permute-start | bytes 442376 | tf_op jit(solution)/shard_map/ppermute | solution.py:201
  448.1 6.4 %collective-permute-start.22 = (bf16[1,64,1152]{2,1,0:T(8,128)(2,1)S(1)}, bf16[1,64,1152]{2,1,0:T(8,128)(2,1)S(1)}, u32[]{:S(2)}, u32[]{:S(2)}) collective-permute-start(bf16[1,64,1152]{2,1,0:T(8,128)(2,1)S(1)} %fusion.191), channel_id=1, source_target_pairs={{0,4},{4,0},{8,12},{12,8},{16,20},{20,16},{24,28},{28,24},{1,5},{5... | collective-permute-start | bytes 442376 | tf_op jit(solution)/shard_map/ppermute | solution.py:172
  449.6 5.3 %collective-permute-start.36 = (bf16[1,64,1152]{2,1,0:T(8,128)(2,1)S(1)}, bf16[1,64,1152]{2,1,0:T(8,128)(2,1)S(1)}, u32[]{:S(2)}, u32[]{:S(2)}) collective-permute-start(bf16[1,64,1152]{2,1,0:T(8,128)(2,1)S(1)} %fusion.194), channel_id=1, source_target_pairs={{0,4},{4,0},{8,12},{12,8},{16,20},{20,16},{24,28},{28,24},{1,5},{5... | collective-permute-start | bytes 442376 | tf_op jit(solution)/shard_map/ppermute | solution.py:172
  (4 other events, 4.6 us)
Sparse Core Ops, SparseCore 0:
  213.3 51.3 all-gather.2
  266.9 56.0 all-gather.4

commit v4 on v3

--- a/solution.py
+++ b/solution.py
@@ -316,9 +316,10 @@
     tokens = query_rows.shape[0]
     head_norm = jnp.transpose(head_norm, (1, 2, 0, 3)).reshape(tokens, heads * value_width)
     projected = jnp.dot(head_norm, output_weight, preferred_element_type=jnp.float32)
+    if by_gather:
+        projected, far_down = tie(projected, far_down)
     attended = sum_lanes(projected.reshape((-1,) + residual.shape))
     if by_gather:
-        attended, far_down = tie(attended, far_down)
         weights = lane_weights(
             {
                 0: (expert_up, expert_down),

time: 469 us -> 448 us (0.955)
  waiting for transfers between devices: 152 us -> 132 us
    ppermute x6, waiting for transfers between devices: 61.9 us -> 16.8 us  [halve(): lax.ppermute(given.astype(jnp.bfloat16), axis, order).astype(jnp.float32)]
    ppermute x3, waiting for transfers between devices: 0.01 us -> 25.2 us  [far_lane(): lax.ppermute(part, 'expert', [(lane, lane ^ lanes // 2) for lane in range...]
    unnamed x65 -> x61, local copies, waits for them, and re-layouts: 21.8 us -> 18.7 us
  transfers between devices with their start and end apart: 42 -> 42, of which waited for: 15 -> 16; matrix products, arithmetic and copies ran while one was open for 35% -> 39% of each run, Pallas kernels for 0% -> 0%
where the time goes in v4:
time: 448 us; the launch traced here: 442 us
  matrix products  142 us (32%)
  waiting for transfers between devices  132 us (29%)
  starting transfers between devices  104 us (23%)
  local copies, waits for them, and re-layouts  32.9 us (7%)
  other arithmetic  15.9 us (4%)
  between operations  15.2 us (3%)
    ppermute x24, starting transfers between devices, sum_line(): lax.ppermute(moving.astype(jnp.bfloat16), 'seq', order).astype(jnp.float32)  77 us
    all_gather x2, waiting for transfers between devices, routed_by_gather(): tokens = lax.all_gather(own, 'seq', axis=0, tiled=True)  48.8 us
    dot_general x8, matrix products, expert_rows(): gate_up = jnp.dot(rows_in, expert_up, preferred_element_type=jnp.float32)  37.7 us
    dot_general x8, matrix products, expert_rows(): jnp.dot(hidden, expert_down, preferred_element_type=jnp.float32)  27.1 us
    ppermute x3, waiting for transfers between devices, far_lane(): lax.ppermute(part, 'expert', [(lane, lane ^ lanes // 2) for lane in range...  25.2 us
    ppermute x24, waiting for transfers between devices, sum_line(): lax.ppermute(moving.astype(jnp.bfloat16), 'seq', order).astype(jnp.float32)  19.7 us
    unnamed x61, local copies, waits for them, and re-layouts  18.7 us
    ppermute x6, waiting for transfers between devices, halve(): lax.ppermute(given.astype(jnp.bfloat16), axis, order).astype(jnp.float32)  16.8 us
  transfers between devices with their start and end apart: 42, of which 16 were waited for; matrix products, arithmetic and copies ran while one was open for 39% of the time, Pallas kernels for 0%

profile of v4, /device:TPU:0, one launch (start us, length us, event | category | flops | bytes accessed | tf_op | source)
XLA Modules:
  0.0 442.1 jit_solution(12898655078117828787)
XLA Ops:
  6.5 5.1 %fusion.225 = (bf16[1,1152,1024]{2,1,0:T(8,128)(2,1)}, bf16[1,1152,1024]{2,1,0:T(8,128)(2,1)}) fusion(bf16[1,2304,1024]{2,1,0:T(8,128)(2,1)} %param.36), kind=kLoop, calls=%fused_computation.394 | loop fusion | bytes 9437184 | tf_op jit(solution)/shard_map/slice | solution.py:300
  11.7 2.9 collective-permute-start
  14.7 2.0 collective-permute-start.2
  21.4 5.8 %multiply_select_fusion = f32[8,8,64,64]{3,2,1,0:T(8,128)S(1)} fusion(f32[8,8,64,128]{3,1,2,0:T(8,128)S(1)} %fusion.34, f32[8,64,8,128]{3,2,1,0:T(8,128)} %bitcast.491, f32[8,8,64]{2,1,0:T(8,128)S(1)} %bitcast.523, f32[8,8,64]{2,1,0:T(8,128)S(1)} %add_rsqrt_fusion.1, f32[8,8,128]{2,1,0:T(8,128)S(1)} %get-tuple-element.131, ...), kind=kOutput, calls=%fused_computation.79 | convolution fusion | flops 204996608 | bytes 5312512 | tf_op jit(solution)/shard_map/hnsd,hntd->hnst/dot_general | solution.py:53
  44.0 2.4 fusion.18
  46.4 4.3 fusion.59
  50.7 5.7 %multiply_subtract_fusion = f32[8,8,128,128]{3,2,1,0:T(8,128)S(1)} fusion(f32[8,8,128]{2,1,0:T(8,128)S(1)} %get-tuple-element.130, f32[128,128]{1,0:T(8,128)S(1)} %fusion.197, f32[8,8,64,256]{3,2,1,0:T(8,128)S(1)} %fusion.18, f32[8,8,64,128]{3,1,2,0:T(8,128)S(1)} %fusion.34, f32[8,64,8,128]{3,2,1,0:T(8,128)S(1)} %bitcast.494, ...), kind=kOutput, calls=%fused_computation.32 | convolution fusion | flops 406323200 | bytes 10649600 | tf_op jit(solution)/shard_map/hncd,hnce->hnde/dot_general | solution.py:73
  66.6 3.2 copy-done.10
  69.8 6.1 %all-to-all-start = ((f32[8,128,256]{2,1,0:T(8,128)}), f32[8,128,256]{2,1,0:T(8,128)}, u32[]{:S(2)}, u32[]{:S(2)}) async-start(f32[8,128,256]{2,1,0:T(8,128)} %copy-done.13), calls=%async_computation | async-start | bytes 2097152 | tf_op jit(solution)/shard_map/all_to_all | solution.py:107
  77.0 2.8 bitcast_dynamic-update-slice_fusion.1
  79.8 4.2 fusion.54
  84.0 2.6 fusion.62
  86.6 2.6 fusion.57
  89.2 11.8 %all-to-all-done = f32[8,128,256]{2,1,0:T(8,128)} async-done(((f32[8,128,256]{2,1,0:T(8,128)}), f32[8,128,256]{2,1,0:T(8,128)}, u32[]{:S(2)}, u32[]{:S(2)}) %all-to-all-start) | async-done | bytes 1048608 | tf_op jit(solution)/shard_map/all_to_all | solution.py:107
  112.8 4.2 all-to-all-start.1
  118.1 10.1 %fusion = f32[8,8,64,256]{3,2,1,0:T(8,128)} fusion(f32[8,8,128,256]{3,2,0,1:T(8,128)} %bitcast_dynamic-update-slice_fusion, f32[8,8,64,128]{3,2,1,0:T(8,128)} %fusion.62, f32[8,64,8,128]{3,2,1,0:T(8,128)} %bitcast.497, f32[8,8,64,128]{3,1,2,0:T(8,128)S(1)} %fusion.34, f32[8,8,64]{2,1,0:T(8,128)S(1)} %add_rsqrt_fusion.2), kind=kOutput, calls=%fused_computation | convolution fusion | flops 806879232 | bytes 18890752 | tf_op jit(solution)/shard_map/hnsd,hnde->hnse/dot_general | solution.py:98
  128.2 2.8 all-to-all-done.1
  130.9 4.7 %multiply_reduce_fusion = (f32[8,8,64]{2,1,0:T(8,128)S(1)}, f32[8,8,64,128]{3,2,1,0:T(8,128)S(1)}) fusion(f32[8,128,128]{2,1,0:T(8,128)} %all-to-all-done.1, f32[8,8,64,256]{3,2,1,0:T(8,128)} %fusion, f32[8,8,64,128]{3,2,1,0:T(8,128)} %fusion.57), kind=kOutput, calls=%fused_computation.61 | convolution fusion | flops 404746240 | bytes 8929280 | tf_op jit(solution)/shard_map/hnsd,hde->hnse/dot_general | solution.py:313
  137.1 4.9 %fusion.87 = f32[512,2304]{1,0:T(8,128)S(1)} fusion(bf16[1024,2304]{1,0:T(8,128)(2,1)} %param.33, bf16[64,8,8,128]{3,2,1,0:T(8,128)(2,1)S(1)} %bitcast.522), kind=kOutput, calls=%fused_computation.133 | convolution fusion | flops 2415919104 | bytes 10485760 | tf_op jit(solution)/shard_map/dot_general | solution.py:318
  142.1 25.2 %collective-permute-done.2 = bf16[1,512,2304]{2,1,0:T(8,128)(2,1)} collective-permute-done((bf16[1,512,2304]{2,1,0:T(8,128)(2,1)}, bf16[1,512,2304]{2,1,0:T(8,128)(2,1)}, u32[]{:S(2)}, u32[]{:S(2)}) %collective-permute-start.2) | collective-permute-done | bytes 2359328 | tf_op jit(solution)/shard_map/ppermute | solution.py:151
  167.5 2.8 collective-permute-done.3
  170.3 1.9 bitcast_add_fusion
  172.3 1.8 collective-permute-start.4
  174.1 13.6 %collective-permute-done.4 = bf16[1,128,2304]{2,1,0:T(8,128)(2,1)S(1)} collective-permute-done((bf16[1,128,2304]{2,1,0:T(8,128)(2,1)S(1)}, bf16[1,128,2304]{2,1,0:T(8,128)(2,1)S(1)}, u32[]{:S(2)}, u32[]{:S(2)}) %collective-permute-start.4) | collective-permute-done | bytes 589856 | tf_op jit(solution)/shard_map/ppermute | solution.py:172
  190.3 3.2 constant_dynamic-update-slice_fusion.2
  193.5 3.3 constant_dynamic-update-slice_fusion.1
  198.0 6.1 %all-to-all-start.2 = ((f32[8,4,128]{2,1,0:T(4,128)}), f32[8,4,128]{2,1,0:T(4,128)S(1)}, u32[]{:S(2)}, u32[]{:S(2)}) async-start(f32[8,4,128]{2,1,0:T(4,128)} %bitcast.64), calls=%async_computation.2 | async-start | bytes 32768 | tf_op jit(solution)/shard_map/all_to_all | solution.py:223
  204.3 6.6 %all-to-all-done.2 = f32[8,4,128]{2,1,0:T(4,128)S(1)} async-done(((f32[8,4,128]{2,1,0:T(4,128)}), f32[8,4,128]{2,1,0:T(4,128)S(1)}, u32[]{:S(2)}, u32[]{:S(2)}) %all-to-all-start.2) | async-done | bytes 16416 | tf_op jit(solution)/shard_map/all_to_all | solution.py:223
  211.8 32.4 %all-gather.3.cloned.1.call-done = bf16[512,2304]{1,0:T(8,128)(2,1)} async-done(((bf16[64,2304]{1,0:T(8,128)(2,1)}), bf16[512,2304]{1,0:T(8,128)(2,1)}) %all-gather.3.cloned.1.call-update) | async-done | bytes 2359312 | tf_op jit(solution)/shard_map/all_gather | solution.py:234
  244.2 5.6 %fusion.12 = f32[512,1024]{1,0:T(8,128)S(1)} fusion(bf16[512,2304]{1,0:T(8,128)(2,1)} %all-gather.3.cloned.1.call-done, bf16[1,2304,1024]{2,1,0:T(8,128)(2,1)} %constant_dynamic-update-slice_fusion.1), kind=kOutput, calls=%fused_computation.12 | convolution fusion | flops 2415919104 | bytes 9175040 | tf_op jit(solution)/shard_map/dot_general | solution.py:138
  249.8 3.4 convolution_convert_fusion.6
  253.1 4.5 %fusion.16 = f32[512,1024]{1,0:T(8,128)S(1)} fusion(bf16[512,2304]{1,0:T(8,128)(2,1)S(1)} %copy-done.22, bf16[1,2304,1024]{2,1,0:T(8,128)(2,1)} %param.36), kind=kOutput, calls=%fused_computation.16 | convolution fusion | flops 2415919104 | bytes 9175040 | tf_op jit(solution)/shard_map/dot_general | solution.py:138
  257.7 3.2 convolution_convert_fusion.7
  260.9 4.5 %fusion.8 = f32[512,1024]{1,0:T(8,128)S(1)} fusion(bf16[512,2304]{1,0:T(8,128)(2,1)S(1)} %copy-done.22, bf16[1,2304,1024]{2,1,0:T(8,128)(2,1)} %collective-permute-done.5), kind=kOutput, calls=%fused_computation.8 | convolution fusion | flops 2415919104 | bytes 9175040 | tf_op jit(solution)/shard_map/dot_general | solution.py:138
  265.4 3.2 convolution_convert_fusion.5
  268.6 4.5 %fusion.4 = f32[512,1024]{1,0:T(8,128)S(1)} fusion(bf16[512,2304]{1,0:T(8,128)(2,1)S(1)} %copy-done.22, bf16[1,2304,1024]{2,1,0:T(8,128)(2,1)} %collective-permute-done.7), kind=kOutput, calls=%fused_computation.4 | convolution fusion | flops 2415919104 | bytes 9175040 | tf_op jit(solution)/shard_map/dot_general | solution.py:138
  273.1 3.7 multiply_add_fusion.1
  280.3 4.1 collective-permute-start.16
  285.8 16.4 %all-gather.5.cloned.1.call-done = bf16[512,2304]{1,0:T(8,128)(2,1)} async-done(((bf16[64,2304]{1,0:T(8,128)(2,1)}), bf16[512,2304]{1,0:T(8,128)(2,1)}) %all-gather.5.cloned.1.call-update) | async-done | bytes 2359312 | tf_op jit(solution)/shard_map/all_gather | solution.py:234
  302.2 5.3 %fusion.10 = f32[512,1024]{1,0:T(8,128)S(1)} fusion(bf16[512,2304]{1,0:T(8,128)(2,1)} %all-gather.5.cloned.1.call-done, bf16[1,2304,1024]{2,1,0:T(8,128)(2,1)} %constant_dynamic-update-slice_fusion.1), kind=kOutput, calls=%fused_computation.10 | convolution fusion | flops 2415919104 | bytes 9175040 | tf_op jit(solution)/shard_map/dot_general | solution.py:138
  307.6 3.4 convolution_convert_fusion.2
  310.9 4.5 %fusion.14 = f32[512,1024]{1,0:T(8,128)S(1)} fusion(bf16[512,2304]{1,0:T(8,128)(2,1)S(1)} %copy-done.23, bf16[1,2304,1024]{2,1,0:T(8,128)(2,1)} %param.36), kind=kOutput, calls=%fused_computation.14 | convolution fusion | flops 2415919104 | bytes 9175040 | tf_op jit(solution)/shard_map/dot_general | solution.py:138
  315.4 3.2 convolution_convert_fusion.3
  318.6 4.5 %fusion.2 = f32[512,1024]{1,0:T(8,128)S(1)} fusion(bf16[512,2304]{1,0:T(8,128)(2,1)S(1)} %copy-done.23, bf16[1,2304,1024]{2,1,0:T(8,128)(2,1)} %collective-permute-done.7), kind=kOutput, calls=%fused_computation.2 | convolution fusion | flops 2415919104 | bytes 9175040 | tf_op jit(solution)/shard_map/dot_general | solution.py:138
  323.1 4.5 %fusion.6 = f32[512,1024]{1,0:T(8,128)S(1)} fusion(bf16[512,2304]{1,0:T(8,128)(2,1)S(1)} %copy-done.23, bf16[1,2304,1024]{2,1,0:T(8,128)(2,1)} %collective-permute-done.5), kind=kOutput, calls=%fused_computation.6 | convolution fusion | flops 2415919104 | bytes 9175040 | tf_op jit(solution)/shard_map/dot_general | solution.py:138
  327.6 3.2 convolution_convert_fusion.1
  330.8 3.7 multiply_add_fusion
  335.5 4.9 %collective-permute-start.30 = (bf16[128,1152]{1,0:T(8,128)(2,1)S(1)}, bf16[128,1152]{1,0:T(8,128)(2,1)S(1)}, u32[]{:S(2)}, u32[]{:S(2)}) collective-permute-start(bf16[128,1152]{1,0:T(8,128)(2,1)S(1)} %get-tuple-element.127), channel_id=1, source_target_pairs={{0,8},{4,12},{1,9},{5,13},{2,10},{6,14},{3,11},{7,15}} | collective-permute-start | bytes 884744 | tf_op jit(solution)/shard_map/ppermute | solution.py:201
  342.1 2.9 collective-permute-done.30
  345.0 4.4 collective-permute-start.17
  349.5 2.1 collective-permute-start.31
  351.6 4.7 %collective-permute-done.17 = bf16[128,1152]{1,0:T(8,128)(2,1)S(1)} collective-permute-done((bf16[128,1152]{1,0:T(8,128)(2,1)S(1)}, bf16[128,1152]{1,0:T(8,128)(2,1)S(1)}, u32[]{:S(2)}, u32[]{:S(2)}) %collective-permute-start.17) | collective-permute-done | bytes 294944 | tf_op jit(solution)/shard_map/ppermute | solution.py:201
  358.1 5.0 %collective-permute-start.18 = (bf16[128,1152]{1,0:T(8,128)(2,1)S(1)}, bf16[128,1152]{1,0:T(8,128)(2,1)S(1)}, u32[]{:S(2)}, u32[]{:S(2)}) collective-permute-start(bf16[128,1152]{1,0:T(8,128)(2,1)S(1)} %get-tuple-element.121), channel_id=1, source_target_pairs={{0,8},{4,12},{8,16},{12,20},{16,24},{20,28},{1,9},{5,13},{9,17},{1... | collective-permute-start | bytes 884744 | tf_op jit(solution)/shard_map/ppermute | solution.py:201
  363.9 5.2 %collective-permute-start.32 = (bf16[128,1152]{1,0:T(8,128)(2,1)S(1)}, bf16[128,1152]{1,0:T(8,128)(2,1)S(1)}, u32[]{:S(2)}, u32[]{:S(2)}) collective-permute-start(bf16[128,1152]{1,0:T(8,128)(2,1)S(1)} %get-tuple-element.125), channel_id=1, source_target_pairs={{0,8},{4,12},{8,16},{12,20},{16,24},{20,28},{1,9},{5,13},{9,17},{1... | collective-permute-start | bytes 884744 | tf_op jit(solution)/shard_map/ppermute | solution.py:201
  370.3 4.6 %collective-permute-start.10 = (bf16[64,1152]{1,0:T(8,128)(2,1)S(1)}, bf16[64,1152]{1,0:T(8,128)(2,1)S(1)}, u32[]{:S(2)}, u32[]{:S(2)}) collective-permute-start(bf16[64,1152]{1,0:T(8,128)(2,1)S(1)} %get-tuple-element.134), channel_id=1, source_target_pairs={{0,8},{4,12},{1,9},{5,13},{2,10},{6,14},{3,11},{7,15}} | collective-permute-start | bytes 442376 | tf_op jit(solution)/shard_map/ppermute | solution.py:201
  375.1 3.2 collective-permute-done.10
  378.3 4.4 collective-permute-start.24
  382.7 4.2 collective-permute-done.24
  388.4 4.4 collective-permute-start.11
  392.8 1.9 collective-permute-start.25
  399.6 23.0 %collective-permute-start.12 = (bf16[64,1152]{1,0:T(8,128)(2,1)S(1)}, bf16[64,1152]{1,0:T(8,128)(2,1)S(1)}, u32[]{:S(2)}, u32[]{:S(2)}) collective-permute-start(bf16[64,1152]{1,0:T(8,128)(2,1)S(1)} %get-tuple-element.132), channel_id=1, source_target_pairs={{0,8},{4,12},{8,16},{12,20},{16,24},{20,28},{1,9},{5,13},{9,17},{1... | collective-permute-start | bytes 442376 | tf_op jit(solution)/shard_map/ppermute | solution.py:201
  422.6 1.9 collective-permute-start.26
  429.6 2.0 collective-permute-done.15
  431.6 2.0 collective-permute-done.29
  (220 shorter events, 75.7 us)
Async XLA Ops:
  6.5 10.2 %copy-start.15 = (f32[512,1024]{1,0:T(8,128)S(1)}, f32[512,1024]{1,0:T(8,128)}, u32[]{:S(2)}) copy-start(f32[512,1024]{1,0:T(8,128)} %param.31) | copy-start | bytes 6291460
  11.7 58.1 %collective-permute-start = (bf16[1,1152,1024]{2,1,0:T(8,128)(2,1)}, bf16[1,1152,1024]{2,1,0:T(8,128)(2,1)}, u32[]{:S(2)}, u32[]{:S(2)}) collective-permute-start(bf16[1,1152,1024]{2,1,0:T(8,128)(2,1)} %get-tuple-element.120), channel_id=1, source_target_pairs={{0,2},{1,3},{2,0},{3,1},{4,6},{5,7},{6,4},{7,5},{8,10},{9,11},{10,... | collective-permute-start | bytes 7077896 | tf_op jit(solution)/shard_map/ppermute | solution.py:151
  14.6 113.5 %collective-permute-start.1 = (bf16[1,1152,1024]{2,1,0:T(8,128)(2,1)}, bf16[1,1152,1024]{2,1,0:T(8,128)(2,1)}, u32[]{:S(2)}, u32[]{:S(2)}) collective-permute-start(bf16[1,1152,1024]{2,1,0:T(8,128)(2,1)} %get-tuple-element.119), channel_id=1, source_target_pairs={{0,2},{1,3},{2,0},{3,1},{4,6},{5,7},{6,4},{7,5},{8,10},{9,11},{10,... | collective-permute-start | bytes 7077896 | tf_op jit(solution)/shard_map/ppermute | solution.py:151
  14.7 152.6 %collective-permute-start.2 = (bf16[1,512,2304]{2,1,0:T(8,128)(2,1)}, bf16[1,512,2304]{2,1,0:T(8,128)(2,1)}, u32[]{:S(2)}, u32[]{:S(2)}) collective-permute-start(bf16[1,512,2304]{2,1,0:T(8,128)(2,1)} %param.37), channel_id=1, source_target_pairs={{0,2},{1,3},{2,0},{3,1},{4,6},{5,7},{6,4},{7,5},{8,10},{9,11},{10,... | collective-permute-start | bytes 7077896 | tf_op jit(solution)/shard_map/ppermute | solution.py:151
  17.2 1.4 copy-start.16
  19.4 1.3 copy-start
  19.4 1.9 copy-start.19
  39.3 1.5 copy-start.17
  41.0 1.6 copy-start.1
  46.4 4.3 copy-start.3
  60.2 1.2 copy-start.18
  61.4 2.1 copy-start.7
  62.1 2.1 copy-start.5
  66.6 3.2 copy-start.10
  69.8 31.3 %all-to-all-start = ((f32[8,128,256]{2,1,0:T(8,128)}), f32[8,128,256]{2,1,0:T(8,128)}, u32[]{:S(2)}, u32[]{:S(2)}) async-start(f32[8,128,256]{2,1,0:T(8,128)} %copy-done.13), calls=%async_computation | async-start | bytes 2097152 | tf_op jit(solution)/shard_map/all_to_all | solution.py:107
  75.9 3.9 copy-start.2
  75.9 3.9 copy-start.6
  79.8 4.2 copy-start.4
  89.2 27.7 %copy-start.9 = (f32[8,128,256]{2,1,0:T(8,128)S(1)}, f32[8,128,256]{2,1,0:T(8,128)}, u32[]{:S(2)}) copy-start(f32[8,128,256]{2,1,0:T(8,128)} %copy-done.8) | copy-start | bytes 3145732
  112.8 18.2 %all-to-all-start.1 = ((f32[8,128,128]{2,1,0:T(8,128)}), f32[8,128,128]{2,1,0:T(8,128)}, u32[]{:S(2)}, u32[]{:S(2)}) async-start(f32[8,128,128]{2,1,0:T(8,128)} %fusion.84), calls=%async_computation.1 | async-start | bytes 1048576 | tf_op jit(solution)/shard_map/all_to_all | solution.py:117
  116.9 127.3 %all-gather.3.cloned.1.call-start = ((), (), s32[]{:S(2)}) async-start(), calls=%async_computation.3 | async-start | bytes 2654208 | tf_op jit(solution)/shard_map/all_gather | solution.py:234
  142.1 25.2 %copy-start.14 = (f32[512,2304]{1,0:T(8,128)}, f32[512,2304]{1,0:T(8,128)S(1)}, u32[]{:S(2)}) copy-start(f32[512,2304]{1,0:T(8,128)S(1)} %fusion.87) | copy-start | bytes 14155780
  167.4 2.9 collective-permute-start.3
  172.3 15.4 %collective-permute-start.4 = (bf16[1,128,2304]{2,1,0:T(8,128)(2,1)S(1)}, bf16[1,128,2304]{2,1,0:T(8,128)(2,1)S(1)}, u32[]{:S(2)}, u32[]{:S(2)}) collective-permute-start(bf16[1,128,2304]{2,1,0:T(8,128)(2,1)S(1)} %dynamic-slice_convert_fusion), channel_id=1, source_target_pairs={{0,2},{1,3},{2,0},{3,1},{4,6},{5,7},{6,4},{7,5},{8,10},{9,11},{10,... | collective-permute-start | bytes 1769480 | tf_op jit(solution)/shard_map/ppermute | solution.py:172
  190.2 70.7 %collective-permute-start.5 = (bf16[1,2304,1024]{2,1,0:T(8,128)(2,1)}, bf16[1,2304,1024]{2,1,0:T(8,128)(2,1)}, u32[]{:S(2)}, u32[]{:S(2)}) collective-permute-start(bf16[1,2304,1024]{2,1,0:T(8,128)(2,1)} %param.36), channel_id=1, source_target_pairs={{0,1},{1,0},{2,3},{3,2},{4,5},{5,4},{6,7},{7,6},{8,9},{9,8},{10,11... | collective-permute-start | bytes 14155784 | tf_op jit(solution)/shard_map/ppermute | solution.py:160
  193.5 3.8 copy-start.20
  193.5 3.8 copy-start.21
  196.8 71.8 %collective-permute-start.7 = (bf16[1,2304,1024]{2,1,0:T(8,128)(2,1)}, bf16[1,2304,1024]{2,1,0:T(8,128)(2,1)}, u32[]{:S(2)}, u32[]{:S(2)}) collective-permute-start(bf16[1,2304,1024]{2,1,0:T(8,128)(2,1)} %constant_dynamic-update-slice_fusion.1), channel_id=1, source_target_pairs={{0,1},{1,0},{2,3},{3,2},{4,5},{5,4},{6,7},{7,6},{8,9},{9,8},{10,11... | collective-permute-start | bytes 14155784 | tf_op jit(solution)/shard_map/ppermute | solution.py:160
  198.0 12.8 %all-to-all-start.2 = ((f32[8,4,128]{2,1,0:T(4,128)}), f32[8,4,128]{2,1,0:T(4,128)S(1)}, u32[]{:S(2)}, u32[]{:S(2)}) async-start(f32[8,4,128]{2,1,0:T(4,128)} %bitcast.64), calls=%async_computation.2 | async-start | bytes 32768 | tf_op jit(solution)/shard_map/all_to_all | solution.py:223
  204.1 98.2 %all-gather.5.cloned.1.call-start = ((), (), s32[]{:S(2)}) async-start(), calls=%async_computation.4 | async-start | bytes 2654208 | tf_op jit(solution)/shard_map/all_gather | solution.py:234
  204.1 61.3 %collective-permute-start.6 = (bf16[1,512,2304]{2,1,0:T(8,128)(2,1)}, bf16[1,512,2304]{2,1,0:T(8,128)(2,1)}, u32[]{:S(2)}, u32[]{:S(2)}) collective-permute-start(bf16[1,512,2304]{2,1,0:T(8,128)(2,1)} %param.37), channel_id=1, source_target_pairs={{0,1},{1,0},{2,3},{3,2},{4,5},{5,4},{6,7},{7,6},{8,9},{9,8},{10,11... | collective-permute-start | bytes 7077896 | tf_op jit(solution)/shard_map/ppermute | solution.py:160
  211.7 61.4 %collective-permute-start.8 = (bf16[1,512,2304]{2,1,0:T(8,128)(2,1)}, bf16[1,512,2304]{2,1,0:T(8,128)(2,1)}, u32[]{:S(2)}, u32[]{:S(2)}) collective-permute-start(bf16[1,512,2304]{2,1,0:T(8,128)(2,1)} %collective-permute-done.2), channel_id=1, source_target_pairs={{0,1},{1,0},{2,3},{3,2},{4,5},{5,4},{6,7},{7,6},{8,9},{9,8},{10,11... | collective-permute-start | bytes 7077896 | tf_op jit(solution)/shard_map/ppermute | solution.py:160
  249.8 3.4 copy-start.22
  277.2 1.4 copy-start.11
  278.7 85.2 %collective-permute-start.9 = (bf16[4,64,1152]{2,1,0:T(8,128)(2,1)S(1)}, bf16[4,64,1152]{2,1,0:T(8,128)(2,1)}, u32[]{:S(2)}, u32[]{:S(2)}) collective-permute-start(bf16[4,64,1152]{2,1,0:T(8,128)(2,1)S(1)} %fusion.123), channel_id=1, source_target_pairs={{0,4},{4,0},{8,12},{12,8},{16,20},{20,16},{24,28},{28,24},{1,5},{5... | collective-permute-start | bytes 1769480 | tf_op jit(solution)/shard_map/ppermute | solution.py:172
  280.3 60.1 %collective-permute-start.16 = (bf16[128,1152]{1,0:T(8,128)(2,1)}, bf16[128,1152]{1,0:T(8,128)(2,1)}, u32[]{:S(2)}, u32[]{:S(2)}) collective-permute-start(bf16[128,1152]{1,0:T(8,128)(2,1)} %get-tuple-element.123), channel_id=1, source_target_pairs={{0,8},{4,12},{1,9},{5,13},{2,10},{6,14},{3,11},{7,15}} | collective-permute-start | bytes 884744 | tf_op jit(solution)/shard_map/ppermute | solution.py:201
  284.4 65.1 %collective-permute-start.19 = (bf16[128,1152]{1,0:T(8,128)(2,1)}, bf16[128,1152]{1,0:T(8,128)(2,1)}, u32[]{:S(2)}, u32[]{:S(2)}) collective-permute-start(bf16[128,1152]{1,0:T(8,128)(2,1)} %get-tuple-element.124), channel_id=1, source_target_pairs={{24,16},{28,20},{25,17},{29,21},{26,18},{30,22},{27,19},{31,23}} | collective-permute-start | bytes 884744 | tf_op jit(solution)/shard_map/ppermute | solution.py:201
  307.5 3.4 copy-start.23
  334.9 35.4 %collective-permute-start.23 = (bf16[4,64,1152]{2,1,0:T(8,128)(2,1)S(1)}, bf16[4,64,1152]{2,1,0:T(8,128)(2,1)S(1)}, u32[]{:S(2)}, u32[]{:S(2)}) collective-permute-start(bf16[4,64,1152]{2,1,0:T(8,128)(2,1)S(1)} %fusion.124), channel_id=1, source_target_pairs={{0,4},{4,0},{8,12},{12,8},{16,20},{20,16},{24,28},{28,24},{1,5},{5... | collective-permute-start | bytes 1769480 | tf_op jit(solution)/shard_map/ppermute | solution.py:172
  335.5 9.5 %collective-permute-start.30 = (bf16[128,1152]{1,0:T(8,128)(2,1)S(1)}, bf16[128,1152]{1,0:T(8,128)(2,1)S(1)}, u32[]{:S(2)}, u32[]{:S(2)}) collective-permute-start(bf16[128,1152]{1,0:T(8,128)(2,1)S(1)} %get-tuple-element.127), channel_id=1, source_target_pairs={{0,8},{4,12},{1,9},{5,13},{2,10},{6,14},{3,11},{7,15}} | collective-permute-start | bytes 884744 | tf_op jit(solution)/shard_map/ppermute | solution.py:201
  340.4 17.7 %collective-permute-start.33 = (bf16[128,1152]{1,0:T(8,128)(2,1)S(1)}, bf16[128,1152]{1,0:T(8,128)(2,1)S(1)}, u32[]{:S(2)}, u32[]{:S(2)}) collective-permute-start(bf16[128,1152]{1,0:T(8,128)(2,1)S(1)} %get-tuple-element.128), channel_id=1, source_target_pairs={{24,16},{28,20},{25,17},{29,21},{26,18},{30,22},{27,19},{31,23}} | collective-permute-start | bytes 884744 | tf_op jit(solution)/shard_map/ppermute | solution.py:201
  345.0 11.3 %collective-permute-start.17 = (bf16[128,1152]{1,0:T(8,128)(2,1)S(1)}, bf16[128,1152]{1,0:T(8,128)(2,1)S(1)}, u32[]{:S(2)}, u32[]{:S(2)}) collective-permute-start(bf16[128,1152]{1,0:T(8,128)(2,1)S(1)} %fusion.132), channel_id=1, source_target_pairs={{0,8},{4,12},{8,16},{12,20},{1,9},{5,13},{9,17},{13,21},{2,10},{6,... | collective-permute-start | bytes 884744 | tf_op jit(solution)/shard_map/ppermute | solution.py:201
  349.5 19.6 %copy-start.12 = (f32[512,1152]{1,0:T(8,128)S(1)}, f32[512,1152]{1,0:T(8,128)}, u32[]{:S(2)}) copy-start(f32[512,1152]{1,0:T(8,128)} %copy-done.11) | copy-start | bytes 7077892
  349.5 13.6 %collective-permute-start.31 = (bf16[128,1152]{1,0:T(8,128)(2,1)S(1)}, bf16[128,1152]{1,0:T(8,128)(2,1)S(1)}, u32[]{:S(2)}, u32[]{:S(2)}) collective-permute-start(bf16[128,1152]{1,0:T(8,128)(2,1)S(1)} %fusion.127), channel_id=1, source_target_pairs={{0,8},{4,12},{8,16},{12,20},{1,9},{5,13},{9,17},{13,21},{2,10},{6,... | collective-permute-start | bytes 884744 | tf_op jit(solution)/shard_map/ppermute | solution.py:201
  357.4 30.2 %collective-permute-start.20 = (bf16[128,1152]{1,0:T(8,128)(2,1)S(1)}, bf16[128,1152]{1,0:T(8,128)(2,1)S(1)}, u32[]{:S(2)}, u32[]{:S(2)}) collective-permute-start(bf16[128,1152]{1,0:T(8,128)(2,1)S(1)} %get-tuple-element.122), channel_id=1, source_target_pairs={{16,8},{20,12},{24,16},{28,20},{17,9},{21,13},{25,17},{29,21},{18,... | collective-permute-start | bytes 884744 | tf_op jit(solution)/shard_map/ppermute | solution.py:201
  358.1 64.5 %collective-permute-start.18 = (bf16[128,1152]{1,0:T(8,128)(2,1)S(1)}, bf16[128,1152]{1,0:T(8,128)(2,1)S(1)}, u32[]{:S(2)}, u32[]{:S(2)}) collective-permute-start(bf16[128,1152]{1,0:T(8,128)(2,1)S(1)} %get-tuple-element.121), channel_id=1, source_target_pairs={{0,8},{4,12},{8,16},{12,20},{16,24},{20,28},{1,9},{5,13},{9,17},{1... | collective-permute-start | bytes 884744 | tf_op jit(solution)/shard_map/ppermute | solution.py:201
  363.2 25.1 %collective-permute-start.34 = (bf16[128,1152]{1,0:T(8,128)(2,1)S(1)}, bf16[128,1152]{1,0:T(8,128)(2,1)S(1)}, u32[]{:S(2)}, u32[]{:S(2)}) collective-permute-start(bf16[128,1152]{1,0:T(8,128)(2,1)S(1)} %get-tuple-element.126), channel_id=1, source_target_pairs={{16,8},{20,12},{24,16},{28,20},{17,9},{21,13},{25,17},{29,21},{18,... | collective-permute-start | bytes 884744 | tf_op jit(solution)/shard_map/ppermute | solution.py:201
  363.9 62.0 %collective-permute-start.32 = (bf16[128,1152]{1,0:T(8,128)(2,1)S(1)}, bf16[128,1152]{1,0:T(8,128)(2,1)S(1)}, u32[]{:S(2)}, u32[]{:S(2)}) collective-permute-start(bf16[128,1152]{1,0:T(8,128)(2,1)S(1)} %get-tuple-element.125), channel_id=1, source_target_pairs={{0,8},{4,12},{8,16},{12,20},{16,24},{20,28},{1,9},{5,13},{9,17},{1... | collective-permute-start | bytes 884744 | tf_op jit(solution)/shard_map/ppermute | solution.py:201
  370.3 7.9 %collective-permute-start.10 = (bf16[64,1152]{1,0:T(8,128)(2,1)S(1)}, bf16[64,1152]{1,0:T(8,128)(2,1)S(1)}, u32[]{:S(2)}, u32[]{:S(2)}) collective-permute-start(bf16[64,1152]{1,0:T(8,128)(2,1)S(1)} %get-tuple-element.134), channel_id=1, source_target_pairs={{0,8},{4,12},{1,9},{5,13},{2,10},{6,14},{3,11},{7,15}} | collective-permute-start | bytes 442376 | tf_op jit(solution)/shard_map/ppermute | solution.py:201
  378.3 8.6 %collective-permute-start.24 = (bf16[64,1152]{1,0:T(8,128)(2,1)S(1)}, bf16[64,1152]{1,0:T(8,128)(2,1)S(1)}, u32[]{:S(2)}, u32[]{:S(2)}) collective-permute-start(bf16[64,1152]{1,0:T(8,128)(2,1)S(1)} %get-tuple-element.138), channel_id=1, source_target_pairs={{0,8},{4,12},{1,9},{5,13},{2,10},{6,14},{3,11},{7,15}} | collective-permute-start | bytes 442376 | tf_op jit(solution)/shard_map/ppermute | solution.py:201
  386.9 5.9 %collective-permute-start.13 = (bf16[64,1152]{1,0:T(8,128)(2,1)S(1)}, bf16[64,1152]{1,0:T(8,128)(2,1)S(1)}, u32[]{:S(2)}, u32[]{:S(2)}) collective-permute-start(bf16[64,1152]{1,0:T(8,128)(2,1)S(1)} %get-tuple-element.135), channel_id=1, source_target_pairs={{24,16},{28,20},{25,17},{29,21},{26,18},{30,22},{27,19},{31,23}} | collective-permute-start | bytes 442376 | tf_op jit(solution)/shard_map/ppermute | solution.py:201
  387.6 9.2 %collective-permute-start.27 = (bf16[64,1152]{1,0:T(8,128)(2,1)S(1)}, bf16[64,1152]{1,0:T(8,128)(2,1)S(1)}, u32[]{:S(2)}, u32[]{:S(2)}) collective-permute-start(bf16[64,1152]{1,0:T(8,128)(2,1)S(1)} %get-tuple-element.139), channel_id=1, source_target_pairs={{24,16},{28,20},{25,17},{29,21},{26,18},{30,22},{27,19},{31,23}} | collective-permute-start | bytes 442376 | tf_op jit(solution)/shard_map/ppermute | solution.py:201
  388.4 7.1 %collective-permute-start.11 = (bf16[64,1152]{1,0:T(8,128)(2,1)S(1)}, bf16[64,1152]{1,0:T(8,128)(2,1)S(1)}, u32[]{:S(2)}, u32[]{:S(2)}) collective-permute-start(bf16[64,1152]{1,0:T(8,128)(2,1)S(1)} %fusion.188), channel_id=1, source_target_pairs={{0,8},{4,12},{8,16},{12,20},{1,9},{5,13},{9,17},{13,21},{2,10},{6,... | collective-permute-start | bytes 442376 | tf_op jit(solution)/shard_map/ppermute | solution.py:201
  392.8 5.2 %collective-permute-start.25 = (bf16[64,1152]{1,0:T(8,128)(2,1)S(1)}, bf16[64,1152]{1,0:T(8,128)(2,1)S(1)}, u32[]{:S(2)}, u32[]{:S(2)}) collective-permute-start(bf16[64,1152]{1,0:T(8,128)(2,1)S(1)} %fusion.182), channel_id=1, source_target_pairs={{0,8},{4,12},{8,16},{12,20},{1,9},{5,13},{9,17},{13,21},{2,10},{6,... | collective-permute-start | bytes 442376 | tf_op jit(solution)/shard_map/ppermute | solution.py:201
  395.4 29.1 %collective-permute-start.21 = (bf16[128,1152]{1,0:T(8,128)(2,1)S(1)}, bf16[128,1152]{1,0:T(8,128)(2,1)S(1)}, u32[]{:S(2)}, u32[]{:S(2)}) collective-permute-start(bf16[128,1152]{1,0:T(8,128)(2,1)S(1)} %fusion.131), channel_id=1, source_target_pairs={{8,0},{12,4},{16,8},{20,12},{24,16},{28,20},{9,1},{13,5},{17,9},{2... | collective-permute-start | bytes 884744 | tf_op jit(solution)/shard_map/ppermute | solution.py:201
  396.8 30.5 %collective-permute-start.35 = (bf16[128,1152]{1,0:T(8,128)(2,1)S(1)}, bf16[128,1152]{1,0:T(8,128)(2,1)S(1)}, u32[]{:S(2)}, u32[]{:S(2)}) collective-permute-start(bf16[128,1152]{1,0:T(8,128)(2,1)S(1)} %fusion.126), channel_id=1, source_target_pairs={{8,0},{12,4},{16,8},{20,12},{24,16},{28,20},{9,1},{13,5},{17,9},{2... | collective-permute-start | bytes 884744 | tf_op jit(solution)/shard_map/ppermute | solution.py:201
  398.1 0.7 collective-permute-start.14
  398.8 0.7 collective-permute-start.28
  399.6 29.1 %collective-permute-start.12 = (bf16[64,1152]{1,0:T(8,128)(2,1)S(1)}, bf16[64,1152]{1,0:T(8,128)(2,1)S(1)}, u32[]{:S(2)}, u32[]{:S(2)}) collective-permute-start(bf16[64,1152]{1,0:T(8,128)(2,1)S(1)} %get-tuple-element.132), channel_id=1, source_target_pairs={{0,8},{4,12},{8,16},{12,20},{16,24},{20,28},{1,9},{5,13},{9,17},{1... | collective-permute-start | bytes 442376 | tf_op jit(solution)/shard_map/ppermute | solution.py:201
  422.6 9.0 %collective-permute-start.26 = (bf16[64,1152]{1,0:T(8,128)(2,1)S(1)}, bf16[64,1152]{1,0:T(8,128)(2,1)S(1)}, u32[]{:S(2)}, u32[]{:S(2)}) collective-permute-start(bf16[64,1152]{1,0:T(8,128)(2,1)S(1)} %get-tuple-element.136), channel_id=1, source_target_pairs={{0,8},{4,12},{8,16},{12,20},{16,24},{20,28},{1,9},{5,13},{9,17},{1... | collective-permute-start | bytes 442376 | tf_op jit(solution)/shard_map/ppermute | solution.py:201
  424.5 7.0 %collective-permute-start.15 = (bf16[64,1152]{1,0:T(8,128)(2,1)S(1)}, bf16[64,1152]{1,0:T(8,128)(2,1)S(1)}, u32[]{:S(2)}, u32[]{:S(2)}) collective-permute-start(bf16[64,1152]{1,0:T(8,128)(2,1)S(1)} %fusion.187), channel_id=1, source_target_pairs={{8,0},{12,4},{16,8},{20,12},{24,16},{28,20},{9,1},{13,5},{17,9},{2... | collective-permute-start | bytes 442376 | tf_op jit(solution)/shard_map/ppermute | solution.py:201
  426.0 7.7 %collective-permute-start.29 = (bf16[64,1152]{1,0:T(8,128)(2,1)S(1)}, bf16[64,1152]{1,0:T(8,128)(2,1)S(1)}, u32[]{:S(2)}, u32[]{:S(2)}) collective-permute-start(bf16[64,1152]{1,0:T(8,128)(2,1)S(1)} %fusion.181), channel_id=1, source_target_pairs={{8,0},{12,4},{16,8},{20,12},{24,16},{28,20},{9,1},{13,5},{17,9},{2... | collective-permute-start | bytes 442376 | tf_op jit(solution)/shard_map/ppermute | solution.py:201
  427.3 6.4 %collective-permute-start.22 = (bf16[1,64,1152]{2,1,0:T(8,128)(2,1)S(1)}, bf16[1,64,1152]{2,1,0:T(8,128)(2,1)S(1)}, u32[]{:S(2)}, u32[]{:S(2)}) collective-permute-start(bf16[1,64,1152]{2,1,0:T(8,128)(2,1)S(1)} %fusion.193), channel_id=1, source_target_pairs={{0,4},{4,0},{8,12},{12,8},{16,20},{20,16},{24,28},{28,24},{1,5},{5... | collective-permute-start | bytes 442376 | tf_op jit(solution)/shard_map/ppermute | solution.py:172
  428.7 5.3 %collective-permute-start.36 = (bf16[1,64,1152]{2,1,0:T(8,128)(2,1)S(1)}, bf16[1,64,1152]{2,1,0:T(8,128)(2,1)S(1)}, u32[]{:S(2)}, u32[]{:S(2)}) collective-permute-start(bf16[1,64,1152]{2,1,0:T(8,128)(2,1)S(1)} %fusion.196), channel_id=1, source_target_pairs={{0,4},{4,0},{8,12},{12,8},{16,20},{20,16},{24,28},{28,24},{1,5},{5... | collective-permute-start | bytes 442376 | tf_op jit(solution)/shard_map/ppermute | solution.py:172
  (2 other events, 2.0 us)
Sparse Core Ops, SparseCore 0:
  190.3 53.8 all-gather.2
  246.4 55.7 all-gather.4
